TPU v7x, 256 devices: a whole 4x4x8 slice. The times are simulated.
256 devices in a mesh: view: 8 (over y, x_hi), seq: 32 (over x_lo, z, core).
Axes of the slice: x: 4 (x_hi: 2, x_lo: 2; x = x_hi * 2 + x_lo), y: 4, z: 8, core: 2. Of those that a mesh axis runs over, the one named last changes fastest.
Arguments:
- queries: bfloat16 [8, 4096, 1536], P('view', 'seq'), may hold values from -10 to 10
- keys: bfloat16 [8, 4096, 1536], P('view', 'seq'), may hold values from -10 to 10
- values: bfloat16 [8, 4096, 1536], P('view', 'seq'), may hold values from -6 to 6
- hidden_in: bfloat16 [8, 4096, 1536], P('view', 'seq'), may hold values from -6 to 6
- gate: float32 [8, 1536], P('view'), may hold values from 0.5 to 1.5
- w_out: bfloat16 [1536, 1536], replicated, may hold values from -0.15625 to 0.15625
Outputs:
- block_out: bfloat16 [8, 4096, 1536], P('view', 'seq')
All inputs are finite; a program needn't handle non-finite values.
Results may differ from a plain program's by a relative error of at most 0.0013.
The roundings to bfloat16 on the way count: a program that leaves them out, or rounds other values in their place, can miss the bound.
Values may be sent and summed in bfloat16 or wider, within the bound.
No kernel may reach another device: no remote copies, remote signals or barrier semaphores. Data moves between devices by JAX's collectives and lax.ppermute only.
A program may use at most 128 MiB of HBM per device.

v0:
```python
import functools
import math

import jax
import jax.numpy as jnp
from jax import lax
from jax.experimental import pallas as pl
from jax.experimental.pallas import tpu as pltpu
from jax.sharding import Mesh, PartitionSpec as P

EXP2_SCALE = math.log2(math.e) / 8.0
VMEM = 32 * 2**20
PREP_PARAMS = pltpu.CompilerParams(vmem_limit_bytes=60 * 2**20)
PARAMS = pltpu.CompilerParams(vmem_limit_bytes=VMEM)
LEAST, MOST = 2.0**-64, 2.0**64
AXES = ("y", "xh", "xl", "z", "core")
SIZES = (4, 2, 2, 8, 2)


def swap_halves(tile):
    return jnp.concatenate([tile[:, 64:], tile[:, :64]], axis=1)


def pair_heads(tile):
    half = tile.shape[0] // 2
    upper, lower = tile[:half], tile[half:]
    first = jnp.concatenate([upper[:, :64], lower[:, :64]], axis=1)
    second = jnp.concatenate([upper[:, 64:], lower[:, 64:]], axis=1)
    return first, second


def prep_kernel(q_ref, k_ref, v_ref, pool_ref, own_ref):
    rows = lax.broadcasted_iota(jnp.int32, (32, 128), 0)
    cols = lax.broadcasted_iota(jnp.int32, (32, 128), 1)
    mean4 = jnp.where(cols // 4 == rows, 0.25, 0.0).astype(jnp.bfloat16)
    for j in range(12):
        span = pl.ds(j * 128, 128)
        q, k, v = q_ref[:, span], k_ref[:, span], v_ref[:, span]
        qt, vt = q.T, v.T
        packed_k = pair_heads(k)
        pooled_k = pair_heads(
            jnp.dot(mean4, k, preferred_element_type=jnp.float32).astype(jnp.bfloat16)
        )
        pooled_v = pair_heads(
            jnp.dot(mean4, v, preferred_element_type=jnp.float32).astype(jnp.bfloat16)
        )
        for side in range(2):
            group, member = divmod(2 * j + side, 3)
            own_ref[group, member, 0:64] = qt[side * 64 : side * 64 + 64]
            own_ref[group, member, 64:128] = packed_k[side]
            own_ref[group, member, 128:192] = vt[side * 64 : side * 64 + 64]
            pool_ref[group, 0, member] = pooled_k[side]
            pool_ref[group, 1, member] = pooled_v[side]


def prep(q, k, v):
    return pl.pallas_call(
        prep_kernel,
        out_shape=(
            jax.ShapeDtypeStruct((8, 2, 3, 16, 128), jnp.bfloat16),
            jax.ShapeDtypeStruct((8, 3, 192, 128), jnp.bfloat16),
        ),
        compiler_params=PREP_PARAMS,
        name="prep",
    )(q, k, v)


def repack_kernel(pool_ref, out_ref):
    for member in range(3):
        out_ref[0, member] = pool_ref[:, 0, member].reshape(128, 128)
        out_ref[1, member] = pool_ref[:, 1, member].reshape(128, 128).T


def repack(pool):
    return pl.pallas_call(
        repack_kernel,
        out_shape=jax.ShapeDtypeStruct((2, 3, 128, 128), jnp.bfloat16),
        name="repack",
    )(pool)


def both_places(qt):
    zero = jnp.zeros_like(qt)
    return jnp.concatenate([qt, zero], axis=0), jnp.concatenate([zero, qt], axis=0)


def score(keys, queries):
    return jnp.dot(keys, queries, preferred_element_type=jnp.float32)


def outside(totals):
    return jnp.logical_not((jnp.min(totals) > LEAST) & (jnp.max(totals) < MOST))


def peak(a):
    return jnp.max(a.reshape(-1, 8, a.shape[1]), axis=0)


def joined(near, far):
    most = jnp.maximum(near[72:73], far[72:73])
    near_by = jnp.exp2((near[72:73] - most) * EXP2_SCALE)
    far_by = jnp.exp2((far[72:73] - most) * EXP2_SCALE)
    return near[0:72] * near_by + far[0:72] * far_by, most


def row_keys(row, head):
    return row[0, :, head].reshape(512, 128)


def row_weighted(row, head, p):
    parts = [row[1, x, head] for x in range(4)]
    values = jnp.concatenate([v[:64] for v in parts] + [v[64:] for v in parts], axis=1)
    ones = jnp.ones((16, 1024), jnp.bfloat16)
    return score(jnp.concatenate([values, ones], axis=0), p)


def cross_head(head, q_ref, rows, out_ref):
    upper, lower = both_places(jnp.concatenate([q_ref[z, head] for z in range(8)], axis=1))
    total = jnp.zeros((80, 1024), jnp.float32)
    for row in rows:
        p = [
            jnp.exp2(score(row_keys(row, head), place) * EXP2_SCALE).astype(jnp.bfloat16)
            for place in (upper, lower)
        ]
        total = total + row_weighted(row, head, jnp.concatenate(p, axis=0))
    out_ref[head, 0:72] = total[0:72]
    out_ref[head, 72:80] = jnp.zeros((8, 1024), jnp.float32)


def cross_shifted(head, q_ref, rows, out_ref):
    def one(i, carry):
        places = both_places(jnp.concatenate([q_ref[2 * i, head], q_ref[2 * i + 1, head]], axis=1))
        span = pl.ds(pl.multiple_of(i * 256, 256), 256)
        ones = jnp.ones((16, 256), jnp.bfloat16)
        out_ref[head, 0:72, span] = jnp.zeros((72, 256), jnp.float32)
        out_ref[head, 72:80, span] = jnp.full((8, 256), -jnp.inf, jnp.float32)
        for row in rows:

            def some(x, carry):
                a = jnp.concatenate([score(row[0, x, head], place) for place in places], axis=0)
                top = out_ref[head, 72:73, span]
                newer = jnp.maximum(top, jnp.max(peak(a), axis=0, keepdims=True))
                p = jnp.exp2((a - newer) * EXP2_SCALE).astype(jnp.bfloat16)
                v = row[1, x, head]
                values = jnp.concatenate([jnp.concatenate([v[:64], v[64:]], axis=1), ones], axis=0)
                total = out_ref[head, 0:72, span] * jnp.exp2((top - newer) * EXP2_SCALE)
                out_ref[head, 0:72, span] = total + score(values, p)[0:72]
                out_ref[head, 72:80, span] = jnp.broadcast_to(newer, (8, 256))
                return carry

            lax.fori_loop(0, 4, some, 0)
        return carry

    lax.fori_loop(0, 4, one, 0)


def each_head(count, step, unroll=False):
    if unroll:
        for head in range(count):
            step(head)
    else:
        lax.fori_loop(0, count, lambda head, carry: (step(head), carry)[1], 0)


def cross_kernel(sides, count, *refs):
    q_refs, rows, rest = refs[:sides], refs[sides : sides + count], refs[sides + count :]
    before_refs, out_refs = rest[:-sides], rest[-sides:]

    def plain(head):
        for side in range(sides):
            cross_head(head, q_refs[side], rows, out_refs[side])

    each_head(3, plain)
    totals = jnp.concatenate([ref[:, 64:65] for ref in out_refs], axis=0)

    @pl.when(outside(totals))
    def _():
        for side in range(sides):
            each_head(3, lambda head: cross_shifted(head, q_refs[side], rows, out_refs[side]))

    def join(head):
        for before_ref, out_ref in zip(before_refs, out_refs):
            whole, most = joined(out_ref[head], before_ref[head])
            out_ref[head, 0:72] = whole
            out_ref[head, 72:80] = jnp.broadcast_to(most, (8, 1024))

    if before_refs:
        each_head(3, join)


def own_keys(kvs, head, block):
    return kvs[block][:, head, 0:64].reshape(512, 128)


def own_values(kvs, head, block):
    return jnp.concatenate([kvs[block][c, head, 64:128] for c in range(8)], axis=1)


def own_finish(head, kvs, near_ref, far_ref, out_ref, p_ref, sums):
    by = 1.0 / sums
    total = jnp.zeros((64, 1024), jnp.float32)
    for block in range(4):
        w = (p_ref[8 * block : 8 * block + 8].reshape(1024, 1024) * by).astype(jnp.bfloat16)
        total = total + score(own_values(kvs, head, block), w)
    whole, _ = joined(near_ref[head], far_ref[head])
    result = (total + whole[0:64] / whole[64:65]).astype(jnp.bfloat16)
    for z in range(8):
        out_ref[z, head] = result[:, 128 * z : 128 * z + 128]


def own_weights(head, q_ref, kvs, p_ref):
    upper, lower = both_places(jnp.concatenate([q_ref[z, head] for z in range(8)], axis=1))
    sums = jnp.zeros((8, 1024), jnp.float32)
    for block in range(4):
        for side, place in enumerate((upper, lower)):
            p = jnp.exp2(score(own_keys(kvs, head, block), place) * EXP2_SCALE)
            p_ref[8 * block : 8 * block + 8, 64 * side : 64 * side + 64] = p.reshape(8, 64, 1024)
            sums = sums + jnp.sum(p.reshape(-1, 8, 1024), axis=0)
    return jnp.sum(sums, axis=0, keepdims=True)


def own_shifted(head, q_ref, kvs, p_ref, sum_ref):
    def one(i, carry):
        span = pl.ds(pl.multiple_of(i * 256, 256), 256)
        places = both_places(jnp.concatenate([q_ref[2 * i, head], q_ref[2 * i + 1, head]], axis=1))
        top = jnp.full((8, 256), -jnp.inf, jnp.float32)
        for block, kv in enumerate(kvs):

            def scored(c, top):
                for side, place in enumerate(places):
                    a = score(kv[c, head, 0:64], place)
                    p_ref[8 * block + c, 64 * side : 64 * side + 64, span] = a
                    top = jnp.maximum(top, peak(a))
                return top

            top = lax.fori_loop(0, 8, scored, top)
        top = jnp.max(top, axis=0, keepdims=True)

        def weighed(c, sums):
            p = jnp.exp2((p_ref[c, :, span] - top) * EXP2_SCALE)
            p_ref[c, :, span] = p
            return sums + jnp.sum(p.reshape(16, 8, 256), axis=0)

        sums = lax.fori_loop(0, 32, weighed, jnp.zeros((8, 256), jnp.float32))
        sum_ref[head, 0:1, span] = jnp.sum(sums, axis=0, keepdims=True)
        return carry

    lax.fori_loop(0, 4, one, 0)


def own_kernel(q_ref, kv0, kv1, kv2, kv3, near_ref, far_ref, out_ref, p_ref, sum_ref):
    kvs = (kv0, kv1, kv2, kv3)
    rest = kvs, near_ref, far_ref, out_ref, p_ref

    def whole(head):
        sum_ref[head, 0:1] = own_weights(head, q_ref, kvs, p_ref)

        @pl.when(outside(sum_ref[head, 0:1]))
        def _():
            own_shifted(head, q_ref, kvs, p_ref, sum_ref)

        own_finish(head, *rest, sum_ref[head, 0:1])

    each_head(3, whole)


def cross_attend(queries, rows, before):
    sides = len(queries)
    sums = jax.ShapeDtypeStruct((3, 80, 1024), jnp.float32)
    return pl.pallas_call(
        functools.partial(cross_kernel, sides, len(rows)),
        out_shape=[sums] * sides,
        compiler_params=PARAMS,
        name="cross",
    )(*queries, *rows, *before)


def own_attend(q, column, near, far):
    return pl.pallas_call(
        own_kernel,
        out_shape=jax.ShapeDtypeStruct((8, 3, 64, 128), jnp.bfloat16),
        scratch_shapes=[
            pltpu.VMEM((32, 128, 1024), jnp.float32),
            pltpu.VMEM((3, 8, 1024), jnp.float32),
        ],
        compiler_params=PARAMS,
        name="own",
    )(q, *column, near, far)


def project_kernel(heads_ref, w_ref, hidden_ref, gate_ref, out_ref):
    rows = jnp.concatenate(
        [heads_ref[128 * j : 128 * j + 128].T for j in range(12)], axis=1
    )
    projected = jnp.dot(rows, w_ref[...], preferred_element_type=jnp.float32)
    out_ref[...] = (hidden_ref[...].astype(jnp.float32) + gate_ref[...] * projected).astype(
        jnp.bfloat16
    )


def project(heads, w_out, hidden, gate):
    return pl.pallas_call(
        project_kernel,
        out_shape=jax.ShapeDtypeStruct((128, 1536), jnp.bfloat16),
        compiler_params=PARAMS,
        name="project",
    )(heads, w_out, hidden, gate)


def shifted(array, axis, size, step):
    return lax.ppermute(array, axis, [(i, (i + step) % size) for i in range(size)])


def body(queries, keys, values, hidden_in, gate, w_out):
    x, y = ("xh", "xl"), "y"
    pool, own = prep(queries[0], keys[0], values[0])
    pool = lax.all_to_all(pool, "z", 0, 0, tiled=True)
    own = lax.all_to_all(own, "z", 0, 0, tiled=True)
    piece = repack(pool)
    row = jnp.stack([piece] + [shifted(piece, x, 4, step) for step in (1, 3, 2)], axis=1)
    back, ahead = shifted(row, y, 4, 1), shifted(row, y, 4, 3)
    across = shifted(back, y, 4, 1)
    q, kv = own[:, :, :64], own[:, :, 64:]
    kv_x = shifted(kv, "xl", 2, 1)
    column = [kv, shifted(kv, "core", 2, 1), kv_x, shifted(kv_x, "core", 2, 1)]
    q_far = shifted(q, "core", 2, 1)
    sums = cross_attend([q_far, q], [row], [])
    sums = cross_attend([q_far, q], [back, ahead], sums)
    (far,) = cross_attend([q_far], [across], sums[:1])
    far = shifted(far, "core", 2, 1)
    (near,) = cross_attend([q], [across], sums[1:])
    heads = own_attend(q, column, near, far)
    returned = lax.all_to_all(heads, "z", 0, 0, tiled=True)
    result = project(returned.reshape(1536, 128), w_out, hidden_in[0], gate)
    return result[None]


def solution(mesh):
    fine = Mesh(mesh.devices.reshape(SIZES), AXES)
    tokens = P(("y", "xh"), ("xl", "z", "core"), None)
    placed = (tokens, tokens, tokens, tokens, P(("y", "xh"), None), P())
    return jax.shard_map(body, mesh=fine, in_specs=placed, out_specs=tokens, check_vma=False)
```

profile of v0, /device:TPU:2, one launch (start us, length us, event | category | flops | bytes accessed | tf_op | source)
XLA Modules:
  0.0 315.6 jit_solution(6511377846907454271)
XLA Ops:
  0.0 2.9 prep.1
  2.9 19.0 %all_to_all.15.pool_ref = bf16[8,2,3,16,128]{4,3,2,1,0:T(8,128)(2,1)} all-to-all(bf16[8,2,3,16,128]{4,3,2,1,0:T(8,128)(2,1)} %get-tuple-element.12), channel_id=1, replica_groups=mesh['y'=4,'xh'=2,'xl'=2,'z'=8,'core'=2] {'z'}, dimensions={0} | all-to-all | bytes 393216 | tf_op jit(solution)/shard_map/all_to_all | solution.py:317
  21.9 4.3 %all-to-all-start = ((bf16[8,3,192,128]{3,2,1,0:T(8,128)(2,1)}), bf16[8,3,192,128]{3,2,1,0:T(8,128)(2,1)}, u32[]{:S(2)}, u32[]{:S(2)}) async-start(bf16[8,3,192,128]{3,2,1,0:T(8,128)(2,1)} %get-tuple-element.11), calls=%async_computation | async-start | bytes 2359296 | tf_op jit(solution)/shard_map/all_to_all | solution.py:318
  26.1 1.7 repack.1
  27.8 1.5 collective-permute-start.3
  29.3 0.5 collective-permute-start.4
  29.9 2.1 collective-permute-start.5
  32.0 3.8 %collective-permute-done.3 = bf16[2,3,128,128]{3,2,1,0:T(8,128)(2,1)S(1)} collective-permute-done((bf16[2,3,128,128]{3,2,1,0:T(8,128)(2,1)}, bf16[2,3,128,128]{3,2,1,0:T(8,128)(2,1)S(1)}, u32[]{:S(2)}, u32[]{:S(2)}) %collective-permute-start.3) | collective-permute-done | bytes 196640 | tf_op jit(solution)/shard_map/ppermute | solution.py:311
  35.8 1.0 collective-permute-done.4
  36.7 2.1 collective-permute-done.5
  38.8 1.0 pad_maximum_fusion.refs_2_
  39.8 1.7 collective-permute-start.6
  41.5 1.7 collective-permute-start.9
  43.2 14.4 %collective-permute-done.6.refs_2_ = bf16[2,4,3,128,128]{4,3,2,1,0:T(8,128)(2,1)S(1)} collective-permute-done((bf16[2,4,3,128,128]{4,3,2,1,0:T(8,128)(2,1)S(1)}, bf16[2,4,3,128,128]{4,3,2,1,0:T(8,128)(2,1)S(1)}, u32[]{:S(2)}, u32[]{:S(2)}) %collective-permute-start.6) | collective-permute-done | bytes 786464 | tf_op jit(solution)/shard_map/ppermute | solution.py:311
  57.5 1.5 collective-permute-start.7
  59.0 0.0 all-to-all-done
  59.1 1.2 slice.9.kv0
  60.3 1.0 collective-permute-start.1
  61.3 1.0 slice.8.refs_1_.refs_0_.q_ref
  62.3 0.1 collective-permute-start.8
  62.4 1.7 collective-permute-done.8.refs_0_
  64.1 40.9 %cross.4 = (f32[3,80,1024]{2,1,0:T(8,128)S(1)}, f32[3,80,1024]{2,1,0:T(8,128)S(1)}) custom-call(bf16[8,3,64,128]{3,2,1,0:T(8,128)(2,1)S(1)} %collective-permute-done.8.refs_0_, bf16[8,3,64,128]{3,2,1,0:T(8,128)(2,1)S(1)} %slice.8.refs_1_.refs_0_.q_ref, bf16[2,4,3,128,128]{4,3,2,1,0:T(8,128)(2,1)S(1)} %pad_maximum_fusion.refs_2_), custom_call_target="tpu_custom_call" | custom-call | tf_op jit(solution)/shard_map/cross/pallas_call | solution.py:270
  105.0 0.0 collective-permute-done.9.refs_3_
  105.0 0.0 slice-start
  105.0 81.6 %cross.5 = (f32[3,80,1024]{2,1,0:T(8,128)S(1)}, f32[3,80,1024]{2,1,0:T(8,128)S(1)}) custom-call(bf16[8,3,64,128]{3,2,1,0:T(8,128)(2,1)S(1)} %collective-permute-done.8.refs_0_, bf16[8,3,64,128]{3,2,1,0:T(8,128)(2,1)S(1)} %slice.8.refs_1_.refs_0_.q_ref, bf16[2,4,3,128,128]{4,3,2,1,0:T(8,128)(2,1)S(1)} %collective-permute-done.6.refs_2_, ...), custom_call_target="tpu_custom_call" | custom-call | tf_op jit(solution)/shard_map/cross/pallas_call | solution.py:270
  186.6 0.0 collective-permute-done.7.refs_1_
  186.6 3.3 %cross.7 = f32[3,80,1024]{2,1,0:T(8,128)S(1)} custom-call(bf16[8,3,64,128]{3,2,1,0:T(8,128)(2,1)S(1)} %collective-permute-done.8.refs_0_, bf16[2,4,3,128,128]{4,3,2,1,0:T(8,128)(2,1)S(1)} %collective-permute-done.7.refs_1_, f32[3,80,1024]{2,1,0:T(8,128)S(1)} %get-tuple-element.16.refs_2_), custom_call_target="tpu_custom_call" | custom-call | tf_op jit(solution)/shard_map/cross/pallas_call | solution.py:270
  190.0 0.1 collective-permute-start.10
  190.1 0.5 collective-permute-start
  190.6 0.0 collective-permute-done.1.kv2
  190.6 0.1 collective-permute-start.2
  190.7 0.0 slice-start.1
  190.7 20.9 %cross.6.near_ref = f32[3,80,1024]{2,1,0:T(8,128)S(1)} custom-call(bf16[8,3,64,128]{3,2,1,0:T(8,128)(2,1)S(1)} %slice.8.refs_1_.refs_0_.q_ref, bf16[2,4,3,128,128]{4,3,2,1,0:T(8,128)(2,1)S(1)} %collective-permute-done.7.refs_1_, f32[3,80,1024]{2,1,0:T(8,128)S(1)} %get-tuple-element.15.refs_2_), custom_call_target="tpu_custom_call" | custom-call | tf_op jit(solution)/shard_map/cross/pallas_call | solution.py:270
  211.5 0.0 copy-start
  211.5 0.0 copy-start.1
  211.6 0.0 collective-permute-done.kv1
  211.6 0.0 collective-permute-done.10.far_ref
  211.6 0.0 collective-permute-done.2.kv3
  211.6 83.8 %own.1 = bf16[8,3,64,128]{3,2,1,0:T(8,128)(2,1)S(1)} custom-call(bf16[8,3,64,128]{3,2,1,0:T(8,128)(2,1)S(1)} %slice.8.refs_1_.refs_0_.q_ref, bf16[8,3,128,128]{3,2,1,0:T(8,128)(2,1)S(1)} %slice.9.kv0, bf16[8,3,128,128]{3,2,1,0:T(8,128)(2,1)S(1)} %collective-permute-done.kv1, bf16[8,3,128,128]{3,2,1,0:T(8,128)(2,1)S(1)} %collective-permute-done.1.kv2, ...), custom_call_target="tpu_custom_call" | custom-call | tf_op jit(solution)/shard_map/own/pallas_call | solution.py:279
  295.4 18.6 %all_to_all.16 = bf16[8,3,64,128]{3,2,1,0:T(8,128)(2,1)S(1)} all-to-all(bf16[8,3,64,128]{3,2,1,0:T(8,128)(2,1)S(1)} %own.1), channel_id=1, replica_groups=mesh['y'=4,'xh'=2,'xl'=2,'z'=8,'core'=2] {'z'}, dimensions={0} | all-to-all | bytes 786432 | tf_op jit(solution)/shard_map/all_to_all | solution.py:333
  314.0 0.0 slice-done
  314.0 0.0 slice-done.1
  314.0 0.0 copy-done
  314.0 0.0 copy-done.1
  314.0 1.6 project.1
  (1 shorter events, 0.0 us)
Async XLA Ops:
  21.9 37.2 %all-to-all-start = ((bf16[8,3,192,128]{3,2,1,0:T(8,128)(2,1)}), bf16[8,3,192,128]{3,2,1,0:T(8,128)(2,1)}, u32[]{:S(2)}, u32[]{:S(2)}) async-start(bf16[8,3,192,128]{3,2,1,0:T(8,128)(2,1)} %get-tuple-element.11), calls=%async_computation | async-start | bytes 2359296 | tf_op jit(solution)/shard_map/all_to_all | solution.py:318
  27.8 7.9 %collective-permute-start.3 = (bf16[2,3,128,128]{3,2,1,0:T(8,128)(2,1)}, bf16[2,3,128,128]{3,2,1,0:T(8,128)(2,1)S(1)}, u32[]{:S(2)}, u32[]{:S(2)}) collective-permute-start(bf16[2,3,128,128]{3,2,1,0:T(8,128)(2,1)} %repack.1), channel_id=1, source_target_pairs={{0,16},{16,32},{32,48},{48,0},{1,17},{17,33},{33,49},{49,1},{2,18}... | collective-permute-start | bytes 589832 | tf_op jit(solution)/shard_map/ppermute | solution.py:311
  29.3 7.4 %collective-permute-start.4 = (bf16[2,3,128,128]{3,2,1,0:T(8,128)(2,1)}, bf16[2,3,128,128]{3,2,1,0:T(8,128)(2,1)S(1)}, u32[]{:S(2)}, u32[]{:S(2)}) collective-permute-start(bf16[2,3,128,128]{3,2,1,0:T(8,128)(2,1)} %repack.1), channel_id=1, source_target_pairs={{0,48},{16,0},{32,16},{48,32},{1,49},{17,1},{33,17},{49,33},{2,50}... | collective-permute-start | bytes 589832 | tf_op jit(solution)/shard_map/ppermute | solution.py:311
  29.9 8.9 %collective-permute-start.5 = (bf16[2,3,128,128]{3,2,1,0:T(8,128)(2,1)}, bf16[2,3,128,128]{3,2,1,0:T(8,128)(2,1)S(1)}, u32[]{:S(2)}, u32[]{:S(2)}) collective-permute-start(bf16[2,3,128,128]{3,2,1,0:T(8,128)(2,1)} %repack.1), channel_id=1, source_target_pairs={{0,32},{16,48},{32,0},{48,16},{1,33},{17,49},{33,1},{49,17},{2,34}... | collective-permute-start | bytes 589832 | tf_op jit(solution)/shard_map/ppermute | solution.py:311
  39.8 17.7 %collective-permute-start.6 = (bf16[2,4,3,128,128]{4,3,2,1,0:T(8,128)(2,1)S(1)}, bf16[2,4,3,128,128]{4,3,2,1,0:T(8,128)(2,1)S(1)}, u32[]{:S(2)}, u32[]{:S(2)}) collective-permute-start(bf16[2,4,3,128,128]{4,3,2,1,0:T(8,128)(2,1)S(1)} %pad_maximum_fusion.refs_2_), channel_id=1, source_target_pairs={{0,64},{64,128},{128,192},{192,0},{1,65},{65,129},{129,193},{193,1... | collective-permute-start | bytes 2359304 | tf_op jit(solution)/shard_map/ppermute | solution.py:311
  41.5 63.5 %collective-permute-start.9 = (bf16[2,4,3,128,128]{4,3,2,1,0:T(8,128)(2,1)S(1)}, bf16[2,4,3,128,128]{4,3,2,1,0:T(8,128)(2,1)S(1)}, u32[]{:S(2)}, u32[]{:S(2)}) collective-permute-start(bf16[2,4,3,128,128]{4,3,2,1,0:T(8,128)(2,1)S(1)} %pad_maximum_fusion.refs_2_), channel_id=1, source_target_pairs={{0,192},{64,0},{128,64},{192,128},{1,193},{65,1},{129,65},{193,129... | collective-permute-start | bytes 2359304 | tf_op jit(solution)/shard_map/ppermute | solution.py:311
  57.5 129.1 %collective-permute-start.7 = (bf16[2,4,3,128,128]{4,3,2,1,0:T(8,128)(2,1)S(1)}, bf16[2,4,3,128,128]{4,3,2,1,0:T(8,128)(2,1)S(1)}, u32[]{:S(2)}, u32[]{:S(2)}) collective-permute-start(bf16[2,4,3,128,128]{4,3,2,1,0:T(8,128)(2,1)S(1)} %collective-permute-done.6.refs_2_), channel_id=1, source_target_pairs={{0,64},{64,128},{128,192},{192,0},{1,65},{65,129},{129,193},{193,1... | collective-permute-start | bytes 2359304 | tf_op jit(solution)/shard_map/ppermute | solution.py:311
  60.3 130.3 %collective-permute-start.1 = (bf16[8,3,128,128]{3,2,1,0:T(8,128)(2,1)S(1)}, bf16[8,3,128,128]{3,2,1,0:T(8,128)(2,1)S(1)}, u32[]{:S(2)}, u32[]{:S(2)}) collective-permute-start(bf16[8,3,128,128]{3,2,1,0:T(8,128)(2,1)S(1)} %slice.9.kv0), channel_id=1, source_target_pairs={{0,16},{16,0},{1,17},{17,1},{2,18},{18,2},{3,19},{19,3},{4,20},{20... | collective-permute-start | bytes 2359304 | tf_op jit(solution)/shard_map/ppermute | solution.py:311
  62.3 1.8 collective-permute-start.8
  105.0 209.0 %slice-start = ((s8[4718592]{0:T(1024)(128)(4,1)}), s8[4194304]{0:T(1024)(128)(4,1)S(1)}, s32[]{:S(2)}) async-start(s8[4718592]{0:T(1024)(128)(4,1)} %bitcast.10), calls=%async_computation.3 | async-start | bytes 8388608
  190.0 21.6 %collective-permute-start.10 = (f32[3,80,1024]{2,1,0:T(8,128)S(1)}, f32[3,80,1024]{2,1,0:T(8,128)S(1)}, u32[]{:S(2)}, u32[]{:S(2)}) collective-permute-start(f32[3,80,1024]{2,1,0:T(8,128)S(1)} %cross.7), channel_id=1, source_target_pairs={{0,1},{1,0},{2,3},{3,2},{4,5},{5,4},{6,7},{7,6},{8,9},{9,8},{10,11... | collective-permute-start | bytes 2949128 | tf_op jit(solution)/shard_map/ppermute | solution.py:311
  190.1 21.5 %collective-permute-start = (bf16[8,3,128,128]{3,2,1,0:T(8,128)(2,1)S(1)}, bf16[8,3,128,128]{3,2,1,0:T(8,128)(2,1)S(1)}, u32[]{:S(2)}, u32[]{:S(2)}) collective-permute-start(bf16[8,3,128,128]{3,2,1,0:T(8,128)(2,1)S(1)} %slice.9.kv0), channel_id=1, source_target_pairs={{0,1},{1,0},{2,3},{3,2},{4,5},{5,4},{6,7},{7,6},{8,9},{9,8},{10,11... | collective-permute-start | bytes 2359304 | tf_op jit(solution)/shard_map/ppermute | solution.py:311
  190.6 21.0 %collective-permute-start.2 = (bf16[8,3,128,128]{3,2,1,0:T(8,128)(2,1)S(1)}, bf16[8,3,128,128]{3,2,1,0:T(8,128)(2,1)S(1)}, u32[]{:S(2)}, u32[]{:S(2)}) collective-permute-start(bf16[8,3,128,128]{3,2,1,0:T(8,128)(2,1)S(1)} %collective-permute-done.1.kv2), channel_id=1, source_target_pairs={{0,1},{1,0},{2,3},{3,2},{4,5},{5,4},{6,7},{7,6},{8,9},{9,8},{10,11... | collective-permute-start | bytes 2359304 | tf_op jit(solution)/shard_map/ppermute | solution.py:311
  190.7 123.3 %slice-start.1 = ((s8[4718592]{0:T(1024)(128)(4,1)}), s8[524288]{0:T(1024)(128)(4,1)S(1)}, s32[]{:S(2)}) async-start(s8[4718592]{0:T(1024)(128)(4,1)} %bitcast.10), calls=%async_computation.4 | async-start | bytes 1048576
  211.5 102.5 %copy-start = (bf16[1,128,1536]{2,1,0:T(8,128)(2,1)S(1)}, bf16[1,128,1536]{2,1,0:T(8,128)(2,1)}, u32[]{:S(2)}) copy-start(bf16[1,128,1536]{2,1,0:T(8,128)(2,1)} %param.9) | copy-start | bytes 1179652
  211.5 102.5 %copy-start.1 = (f32[1,1536]{1,0:T(1,128)S(1)}, f32[1,1536]{1,0:T(1,128)}, u32[]{:S(2)}) copy-start(f32[1,1536]{1,0:T(1,128)} %gate_ref.1) | copy-start | bytes 18436
where the time goes:
time: 316 us
  Pallas kernels  237 us (75%)
  blocking collectives  37.6 us (12%)
  waiting for transfers between devices  22.9 us (7%)
  starting transfers between devices  15 us (5%)
    pallas_call x4, Pallas kernels, cross_attend(): pl.pallas_call(functools.partial(cross_kernel, sides, len(rows)), out_sha...  147 us
    pallas_call x1, Pallas kernels, own_attend(): pl.pallas_call(own_kernel, out_shape=jax.ShapeDtypeStruct((8, 3, 64, 128)...  83.8 us
    ppermute x11, waiting for transfers between devices, shifted(): lax.ppermute(array, axis, [(i, (i + step) % size) for i in range(size)])  22.9 us
    all_to_all x1, blocking collectives, body(): pool = lax.all_to_all(pool, 'z', 0, 0, tiled=True)  19 us
    all_to_all x1, blocking collectives, body(): returned = lax.all_to_all(heads, 'z', 0, 0, tiled=True)  18.6 us
    ppermute x11, starting transfers between devices, shifted(): lax.ppermute(array, axis, [(i, (i + step) % size) for i in range(size)])  10.8 us
  transfers between devices with their start and end apart: 12, of which 5 were waited for; matrix products, arithmetic and copies ran while one was open for 1% of the time, Pallas kernels for 47%

commit v1 on v0

--- a/solution.py
+++ b/solution.py
@@ -9,7 +9,8 @@
 from jax.sharding import Mesh, PartitionSpec as P
 
 EXP2_SCALE = math.log2(math.e) / 8.0
-VMEM = 32 * 2**20
+VMEM = 20 * 2**20
+OWN_PARAMS = pltpu.CompilerParams(vmem_limit_bytes=32 * 2**20)
 PREP_PARAMS = pltpu.CompilerParams(vmem_limit_bytes=60 * 2**20)
 PARAMS = pltpu.CompilerParams(vmem_limit_bytes=VMEM)
 LEAST, MOST = 2.0**-64, 2.0**64
@@ -75,6 +76,7 @@
     return pl.pallas_call(
         repack_kernel,
         out_shape=jax.ShapeDtypeStruct((2, 3, 128, 128), jnp.bfloat16),
+        compiler_params=PARAMS,
         name="repack",
     )(pool)
 
@@ -162,29 +164,22 @@
         lax.fori_loop(0, count, lambda head, carry: (step(head), carry)[1], 0)
 
 
-def cross_kernel(sides, count, *refs):
-    q_refs, rows, rest = refs[:sides], refs[sides : sides + count], refs[sides + count :]
-    before_refs, out_refs = rest[:-sides], rest[-sides:]
-
-    def plain(head):
-        for side in range(sides):
-            cross_head(head, q_refs[side], rows, out_refs[side])
-
-    each_head(3, plain)
-    totals = jnp.concatenate([ref[:, 64:65] for ref in out_refs], axis=0)
-
-    @pl.when(outside(totals))
+def cross_kernel(count, has_before, has_token, q_ref, *refs):
+    rows, out_ref = refs[:count], refs[-1]
+    if has_token:
+        refs[-2][...] = jnp.zeros((8, 128), jnp.float32)
+    each_head(3, lambda head: cross_head(head, q_ref, rows, out_ref))
+
+    @pl.when(outside(out_ref[:, 64:65]))
     def _():
-        for side in range(sides):
-            each_head(3, lambda head: cross_shifted(head, q_refs[side], rows, out_refs[side]))
+        each_head(3, lambda head: cross_shifted(head, q_ref, rows, out_ref))
 
     def join(head):
-        for before_ref, out_ref in zip(before_refs, out_refs):
-            whole, most = joined(out_ref[head], before_ref[head])
-            out_ref[head, 0:72] = whole
-            out_ref[head, 72:80] = jnp.broadcast_to(most, (8, 1024))
-
-    if before_refs:
+        whole, most = joined(out_ref[head], refs[count][head])
+        out_ref[head, 0:72] = whole
+        out_ref[head, 72:80] = jnp.broadcast_to(most, (8, 1024))
+
+    if has_before:
         each_head(3, join)
 
 
@@ -264,15 +259,32 @@
     each_head(3, whole)
 
 
-def cross_attend(queries, rows, before):
-    sides = len(queries)
-    sums = jax.ShapeDtypeStruct((3, 80, 1024), jnp.float32)
-    return pl.pallas_call(
-        functools.partial(cross_kernel, sides, len(rows)),
-        out_shape=[sums] * sides,
+def cross_attend(q, rows, before=None, wait=None, token=False):
+    others = [array for array in (before, wait) if array is not None]
+    return pl.pallas_call(
+        functools.partial(cross_kernel, len(rows), before is not None, token),
+        out_shape=[jax.ShapeDtypeStruct((8, 128), jnp.float32)] * token
+        + [jax.ShapeDtypeStruct((3, 80, 1024), jnp.float32)],
         compiler_params=PARAMS,
         name="cross",
-    )(*queries, *rows, *before)
+    )(q, *rows, *others)
+
+
+def split_kernel(own_ref, q_ref, kv_ref):
+    q_ref[...] = own_ref[:, :, 0:64]
+    kv_ref[...] = own_ref[:, :, 64:192]
+
+
+def split(own):
+    return pl.pallas_call(
+        split_kernel,
+        out_shape=(
+            jax.ShapeDtypeStruct((8, 3, 64, 128), jnp.bfloat16),
+            jax.ShapeDtypeStruct((8, 3, 128, 128), jnp.bfloat16),
+        ),
+        compiler_params=PARAMS,
+        name="split",
+    )(own)
 
 
 def own_attend(q, column, near, far):
@@ -283,7 +295,7 @@
             pltpu.VMEM((32, 128, 1024), jnp.float32),
             pltpu.VMEM((3, 8, 1024), jnp.float32),
         ],
-        compiler_params=PARAMS,
+        compiler_params=OWN_PARAMS,
         name="own",
     )(q, *column, near, far)
 
@@ -320,15 +332,15 @@
     row = jnp.stack([piece] + [shifted(piece, x, 4, step) for step in (1, 3, 2)], axis=1)
     back, ahead = shifted(row, y, 4, 1), shifted(row, y, 4, 3)
     across = shifted(back, y, 4, 1)
-    q, kv = own[:, :, :64], own[:, :, 64:]
+    q, kv = split(own)
     kv_x = shifted(kv, "xl", 2, 1)
     column = [kv, shifted(kv, "core", 2, 1), kv_x, shifted(kv_x, "core", 2, 1)]
     q_far = shifted(q, "core", 2, 1)
-    sums = cross_attend([q_far, q], [row], [])
-    sums = cross_attend([q_far, q], [back, ahead], sums)
-    (far,) = cross_attend([q_far], [across], sums[:1])
+    token, near = cross_attend(q, [row, back, ahead], token=True)
+    (far,) = cross_attend(q_far, [row, back, ahead], wait=token)
+    token, far = cross_attend(q_far, [across], before=far, token=True)
     far = shifted(far, "core", 2, 1)
-    (near,) = cross_attend([q], [across], sums[1:])
+    (near,) = cross_attend(q, [across], before=near, wait=token)
     heads = own_attend(q, column, near, far)
     returned = lax.all_to_all(heads, "z", 0, 0, tiled=True)
     result = project(returned.reshape(1536, 128), w_out, hidden_in[0], gate)

time: 316 us -> 258 us (0.82)
  Pallas kernels: 237 us -> 185 us
    pallas_call x4 -> x5, Pallas kernels: 147 us -> 96.4 us  [the longest x4 96.4 us: cross_attend(): pl.pallas_call(functools.partial(cross_kernel, len(rows), before is not N...]
  transfers between devices with their start and end apart: 12 -> 12, of which waited for: 5 -> 4; matrix products, arithmetic and copies ran while one was open for 1% -> 0% of each run, Pallas kernels for 47% -> 37%
where the time goes in v1:
time: 258 us
  Pallas kernels  185 us (72%)
  blocking collectives  37.4 us (14%)
  waiting for transfers between devices  21.1 us (8%)
  starting transfers between devices  14.3 us (6%)
    pallas_call x4, Pallas kernels, cross_attend(): pl.pallas_call(functools.partial(cross_kernel, len(rows), before is not N...  96.4 us
    pallas_call x1, Pallas kernels, own_attend(): pl.pallas_call(own_kernel, out_shape=jax.ShapeDtypeStruct((8, 3, 64, 128)...  83.9 us
    ppermute x11, waiting for transfers between devices, shifted(): lax.ppermute(array, axis, [(i, (i + step) % size) for i in range(size)])  21.1 us
    all_to_all x1, blocking collectives, body(): pool = lax.all_to_all(pool, 'z', 0, 0, tiled=True)  18.9 us
    all_to_all x1, blocking collectives, body(): returned = lax.all_to_all(heads, 'z', 0, 0, tiled=True)  18.5 us
    ppermute x11, starting transfers between devices, shifted(): lax.ppermute(array, axis, [(i, (i + step) % size) for i in range(size)])  10.7 us
  transfers between devices with their start and end apart: 12, of which 4 were waited for; matrix products, arithmetic and copies ran while one was open for 0% of the time, Pallas kernels for 37%

profile of v1, /device:TPU:2, one launch (start us, length us, event | category | flops | bytes accessed | tf_op | source)
XLA Modules:
  0.0 257.9 jit_solution(14722411312147784784)
XLA Ops:
  0.0 2.8 %prep.1 = (bf16[8,2,3,16,128]{4,3,2,1,0:T(8,128)(2,1)}, bf16[8,3,192,128]{3,2,1,0:T(8,128)(2,1)}) custom-call(bf16[128,1536]{1,0:T(8,128)(2,1)} %bitcast.15, bf16[128,1536]{1,0:T(8,128)(2,1)} %bitcast.16, bf16[128,1536]{1,0:T(8,128)(2,1)} %bitcast.17), custom_call_target="tpu_custom_call" | custom-call | tf_op jit(solution)/shard_map/prep/pallas_call | solution.py:58
  2.8 18.9 %all_to_all.15.pool_ref = bf16[8,2,3,16,128]{4,3,2,1,0:T(8,128)(2,1)S(1)} all-to-all(bf16[8,2,3,16,128]{4,3,2,1,0:T(8,128)(2,1)} %get-tuple-element.16), channel_id=1, replica_groups=mesh['y'=4,'xh'=2,'xl'=2,'z'=8,'core'=2] {'z'}, dimensions={0} | all-to-all | bytes 393216 | tf_op jit(solution)/shard_map/all_to_all | solution.py:329
  21.8 3.6 %all-to-all-start = ((bf16[8,3,192,128]{3,2,1,0:T(8,128)(2,1)}), bf16[8,3,192,128]{3,2,1,0:T(8,128)(2,1)S(1)}, u32[]{:S(2)}, u32[]{:S(2)}) async-start(bf16[8,3,192,128]{3,2,1,0:T(8,128)(2,1)} %get-tuple-element.13), calls=%async_computation | async-start | bytes 2359296 | tf_op jit(solution)/shard_map/all_to_all | solution.py:330
  25.4 0.1 repack.1
  25.4 1.6 collective-permute-start.3
  27.0 0.5 collective-permute-start.4
  27.5 2.1 collective-permute-start.5
  29.7 3.5 %collective-permute-done.3 = bf16[2,3,128,128]{3,2,1,0:T(8,128)(2,1)S(1)} collective-permute-done((bf16[2,3,128,128]{3,2,1,0:T(8,128)(2,1)S(1)}, bf16[2,3,128,128]{3,2,1,0:T(8,128)(2,1)S(1)}, u32[]{:S(2)}, u32[]{:S(2)}) %collective-permute-start.3) | collective-permute-done | bytes 196640 | tf_op jit(solution)/shard_map/ppermute | solution.py:323
  33.2 1.0 collective-permute-done.4
  34.2 2.1 collective-permute-done.5
  36.3 0.1 pad_maximum_fusion.refs_0_
  36.4 1.7 collective-permute-start.6
  38.0 1.7 collective-permute-start.8
  39.7 14.5 %collective-permute-done.6.refs_1_ = bf16[2,4,3,128,128]{4,3,2,1,0:T(8,128)(2,1)S(1)} collective-permute-done((bf16[2,4,3,128,128]{4,3,2,1,0:T(8,128)(2,1)S(1)}, bf16[2,4,3,128,128]{4,3,2,1,0:T(8,128)(2,1)S(1)}, u32[]{:S(2)}, u32[]{:S(2)}) %collective-permute-start.6) | collective-permute-done | bytes 786464 | tf_op jit(solution)/shard_map/ppermute | solution.py:323
  54.2 1.5 collective-permute-start.7
  55.6 0.0 all-to-all-done.own_ref
  55.6 0.1 split.1
  55.7 1.0 collective-permute-start.1
  56.7 0.0 collective-permute-start.9
  56.7 0.0 collective-permute-done.8.refs_2_
  56.7 62.1 %cross.4 = (f32[8,128]{1,0:T(8,128)S(1)}, f32[3,80,1024]{2,1,0:T(8,128)S(1)}) custom-call(bf16[8,3,64,128]{3,2,1,0:T(8,128)(2,1)S(1)} %get-tuple-element.14.q_ref, bf16[2,4,3,128,128]{4,3,2,1,0:T(8,128)(2,1)S(1)} %pad_maximum_fusion.refs_0_, bf16[2,4,3,128,128]{4,3,2,1,0:T(8,128)(2,1)S(1)} %collective-permute-done.6.refs_1_, ...), custom_call_target="tpu_custom_call" | custom-call | tf_op jit(solution)/shard_map/cross/pallas_call | solution.py:264
  118.8 0.0 collective-permute-done.9.q_ref
  118.8 0.0 slice-start
  118.8 10.1 %cross.5.refs_1_ = f32[3,80,1024]{2,1,0:T(8,128)S(1)} custom-call(bf16[8,3,64,128]{3,2,1,0:T(8,128)(2,1)S(1)} %collective-permute-done.9.q_ref, bf16[2,4,3,128,128]{4,3,2,1,0:T(8,128)(2,1)S(1)} %pad_maximum_fusion.refs_0_, bf16[2,4,3,128,128]{4,3,2,1,0:T(8,128)(2,1)S(1)} %collective-permute-done.6.refs_1_, ...), custom_call_target="tpu_custom_call" | custom-call | tf_op jit(solution)/shard_map/cross/pallas_call | solution.py:264
  128.9 0.0 collective-permute-done.7.refs_0_
  128.9 3.4 %cross.6 = (f32[8,128]{1,0:T(8,128)S(1)}, f32[3,80,1024]{2,1,0:T(8,128)S(1)}) custom-call(bf16[8,3,64,128]{3,2,1,0:T(8,128)(2,1)S(1)} %collective-permute-done.9.q_ref, bf16[2,4,3,128,128]{4,3,2,1,0:T(8,128)(2,1)S(1)} %collective-permute-done.7.refs_0_, f32[3,80,1024]{2,1,0:T(8,128)S(1)} %cross.5.refs_1_), custom_call_target="tpu_custom_call" | custom-call | tf_op jit(solution)/shard_map/cross/pallas_call | solution.py:264
  132.3 0.1 collective-permute-start.10
  132.4 0.5 collective-permute-start
  132.9 0.0 collective-permute-done.1.kv2
  132.9 0.1 collective-permute-start.2
  133.0 0.0 slice-start.1
  133.0 20.9 %cross.7.near_ref = f32[3,80,1024]{2,1,0:T(8,128)S(1)} custom-call(bf16[8,3,64,128]{3,2,1,0:T(8,128)(2,1)S(1)} %get-tuple-element.14.q_ref, bf16[2,4,3,128,128]{4,3,2,1,0:T(8,128)(2,1)S(1)} %collective-permute-done.7.refs_0_, f32[3,80,1024]{2,1,0:T(8,128)S(1)} %get-tuple-element.17.refs_1_, f32[8,128]{1,0:T(8,128)S(1)} %get-tuple-element.19.refs_2_), custom_call_target="tpu_custom_call" | custom-call | tf_op jit(solution)/shard_map/cross/pallas_call | solution.py:264
  153.9 0.0 copy-start
  153.9 0.0 copy-start.1
  153.9 0.0 collective-permute-done.kv1
  153.9 0.0 collective-permute-done.10.far_ref
  153.9 0.0 collective-permute-done.2.kv3
  153.9 83.9 %own.1 = bf16[8,3,64,128]{3,2,1,0:T(8,128)(2,1)S(1)} custom-call(bf16[8,3,64,128]{3,2,1,0:T(8,128)(2,1)S(1)} %get-tuple-element.14.q_ref, bf16[8,3,128,128]{3,2,1,0:T(8,128)(2,1)S(1)} %get-tuple-element.15.kv0, bf16[8,3,128,128]{3,2,1,0:T(8,128)(2,1)S(1)} %collective-permute-done.kv1, bf16[8,3,128,128]{3,2,1,0:T(8,128)(2,1)S(1)} %collective-permute-done.1.kv2, ...), custom_call_target="tpu_custom_call" | custom-call | tf_op jit(solution)/shard_map/own/pallas_call | solution.py:291
  237.8 18.5 %all_to_all.16 = bf16[8,3,64,128]{3,2,1,0:T(8,128)(2,1)S(1)} all-to-all(bf16[8,3,64,128]{3,2,1,0:T(8,128)(2,1)S(1)} %own.1), channel_id=1, replica_groups=mesh['y'=4,'xh'=2,'xl'=2,'z'=8,'core'=2] {'z'}, dimensions={0} | all-to-all | bytes 786432 | tf_op jit(solution)/shard_map/all_to_all | solution.py:345
  256.3 0.0 slice-done
  256.3 0.0 slice-done.1
  256.3 0.0 copy-done
  256.3 0.0 copy-done.1
  256.3 1.6 project.1
  (1 shorter events, 0.0 us)
Async XLA Ops:
  21.8 33.9 %all-to-all-start = ((bf16[8,3,192,128]{3,2,1,0:T(8,128)(2,1)}), bf16[8,3,192,128]{3,2,1,0:T(8,128)(2,1)S(1)}, u32[]{:S(2)}, u32[]{:S(2)}) async-start(bf16[8,3,192,128]{3,2,1,0:T(8,128)(2,1)} %get-tuple-element.13), calls=%async_computation | async-start | bytes 2359296 | tf_op jit(solution)/shard_map/all_to_all | solution.py:330
  25.4 7.8 %collective-permute-start.3 = (bf16[2,3,128,128]{3,2,1,0:T(8,128)(2,1)S(1)}, bf16[2,3,128,128]{3,2,1,0:T(8,128)(2,1)S(1)}, u32[]{:S(2)}, u32[]{:S(2)}) collective-permute-start(bf16[2,3,128,128]{3,2,1,0:T(8,128)(2,1)S(1)} %repack.1), channel_id=1, source_target_pairs={{0,16},{16,32},{32,48},{48,0},{1,17},{17,33},{33,49},{49,1},{2,18}... | collective-permute-start | bytes 589832 | tf_op jit(solution)/shard_map/ppermute | solution.py:323
  27.0 7.2 %collective-permute-start.4 = (bf16[2,3,128,128]{3,2,1,0:T(8,128)(2,1)S(1)}, bf16[2,3,128,128]{3,2,1,0:T(8,128)(2,1)S(1)}, u32[]{:S(2)}, u32[]{:S(2)}) collective-permute-start(bf16[2,3,128,128]{3,2,1,0:T(8,128)(2,1)S(1)} %repack.1), channel_id=1, source_target_pairs={{0,48},{16,0},{32,16},{48,32},{1,49},{17,1},{33,17},{49,33},{2,50}... | collective-permute-start | bytes 589832 | tf_op jit(solution)/shard_map/ppermute | solution.py:323
  27.5 8.7 %collective-permute-start.5 = (bf16[2,3,128,128]{3,2,1,0:T(8,128)(2,1)S(1)}, bf16[2,3,128,128]{3,2,1,0:T(8,128)(2,1)S(1)}, u32[]{:S(2)}, u32[]{:S(2)}) collective-permute-start(bf16[2,3,128,128]{3,2,1,0:T(8,128)(2,1)S(1)} %repack.1), channel_id=1, source_target_pairs={{0,32},{16,48},{32,0},{48,16},{1,33},{17,49},{33,1},{49,17},{2,34}... | collective-permute-start | bytes 589832 | tf_op jit(solution)/shard_map/ppermute | solution.py:323
  36.4 17.8 %collective-permute-start.6 = (bf16[2,4,3,128,128]{4,3,2,1,0:T(8,128)(2,1)S(1)}, bf16[2,4,3,128,128]{4,3,2,1,0:T(8,128)(2,1)S(1)}, u32[]{:S(2)}, u32[]{:S(2)}) collective-permute-start(bf16[2,4,3,128,128]{4,3,2,1,0:T(8,128)(2,1)S(1)} %pad_maximum_fusion.refs_0_), channel_id=1, source_target_pairs={{0,64},{64,128},{128,192},{192,0},{1,65},{65,129},{129,193},{193,1... | collective-permute-start | bytes 2359304 | tf_op jit(solution)/shard_map/ppermute | solution.py:323
  38.0 18.7 %collective-permute-start.8 = (bf16[2,4,3,128,128]{4,3,2,1,0:T(8,128)(2,1)S(1)}, bf16[2,4,3,128,128]{4,3,2,1,0:T(8,128)(2,1)}, u32[]{:S(2)}, u32[]{:S(2)}) collective-permute-start(bf16[2,4,3,128,128]{4,3,2,1,0:T(8,128)(2,1)S(1)} %pad_maximum_fusion.refs_0_), channel_id=1, source_target_pairs={{0,192},{64,0},{128,64},{192,128},{1,193},{65,1},{129,65},{193,129... | collective-permute-start | bytes 2359304 | tf_op jit(solution)/shard_map/ppermute | solution.py:323
  54.2 74.7 %collective-permute-start.7 = (bf16[2,4,3,128,128]{4,3,2,1,0:T(8,128)(2,1)S(1)}, bf16[2,4,3,128,128]{4,3,2,1,0:T(8,128)(2,1)S(1)}, u32[]{:S(2)}, u32[]{:S(2)}) collective-permute-start(bf16[2,4,3,128,128]{4,3,2,1,0:T(8,128)(2,1)S(1)} %collective-permute-done.6.refs_1_), channel_id=1, source_target_pairs={{0,64},{64,128},{128,192},{192,0},{1,65},{65,129},{129,193},{193,1... | collective-permute-start | bytes 2359304 | tf_op jit(solution)/shard_map/ppermute | solution.py:323
  55.7 77.2 %collective-permute-start.1 = (bf16[8,3,128,128]{3,2,1,0:T(8,128)(2,1)S(1)}, bf16[8,3,128,128]{3,2,1,0:T(8,128)(2,1)S(1)}, u32[]{:S(2)}, u32[]{:S(2)}) collective-permute-start(bf16[8,3,128,128]{3,2,1,0:T(8,128)(2,1)S(1)} %get-tuple-element.15.kv0), channel_id=1, source_target_pairs={{0,16},{16,0},{1,17},{17,1},{2,18},{18,2},{3,19},{19,3},{4,20},{20... | collective-permute-start | bytes 2359304 | tf_op jit(solution)/shard_map/ppermute | solution.py:323
  56.7 62.1 %collective-permute-start.9 = (bf16[8,3,64,128]{3,2,1,0:T(8,128)(2,1)S(1)}, bf16[8,3,64,128]{3,2,1,0:T(8,128)(2,1)S(1)}, u32[]{:S(2)}, u32[]{:S(2)}) collective-permute-start(bf16[8,3,64,128]{3,2,1,0:T(8,128)(2,1)S(1)} %get-tuple-element.14.q_ref), channel_id=1, source_target_pairs={{0,1},{1,0},{2,3},{3,2},{4,5},{5,4},{6,7},{7,6},{8,9},{9,8},{10,11... | collective-permute-start | bytes 1179656 | tf_op jit(solution)/shard_map/ppermute | solution.py:323
  118.8 137.5 %slice-start = ((s8[4718592]{0:T(1024)(128)(4,1)}), s8[4194304]{0:T(1024)(128)(4,1)S(1)}, s32[]{:S(2)}) async-start(s8[4718592]{0:T(1024)(128)(4,1)} %bitcast.10), calls=%async_computation.3 | async-start | bytes 8388608
  132.3 21.6 %collective-permute-start.10 = (f32[3,80,1024]{2,1,0:T(8,128)S(1)}, f32[3,80,1024]{2,1,0:T(8,128)S(1)}, u32[]{:S(2)}, u32[]{:S(2)}) collective-permute-start(f32[3,80,1024]{2,1,0:T(8,128)S(1)} %get-tuple-element.20), channel_id=1, source_target_pairs={{0,1},{1,0},{2,3},{3,2},{4,5},{5,4},{6,7},{7,6},{8,9},{9,8},{10,11... | collective-permute-start | bytes 2949128 | tf_op jit(solution)/shard_map/ppermute | solution.py:323
  132.4 21.5 %collective-permute-start = (bf16[8,3,128,128]{3,2,1,0:T(8,128)(2,1)S(1)}, bf16[8,3,128,128]{3,2,1,0:T(8,128)(2,1)S(1)}, u32[]{:S(2)}, u32[]{:S(2)}) collective-permute-start(bf16[8,3,128,128]{3,2,1,0:T(8,128)(2,1)S(1)} %get-tuple-element.15.kv0), channel_id=1, source_target_pairs={{0,1},{1,0},{2,3},{3,2},{4,5},{5,4},{6,7},{7,6},{8,9},{9,8},{10,11... | collective-permute-start | bytes 2359304 | tf_op jit(solution)/shard_map/ppermute | solution.py:323
  132.9 21.0 %collective-permute-start.2 = (bf16[8,3,128,128]{3,2,1,0:T(8,128)(2,1)S(1)}, bf16[8,3,128,128]{3,2,1,0:T(8,128)(2,1)S(1)}, u32[]{:S(2)}, u32[]{:S(2)}) collective-permute-start(bf16[8,3,128,128]{3,2,1,0:T(8,128)(2,1)S(1)} %collective-permute-done.1.kv2), channel_id=1, source_target_pairs={{0,1},{1,0},{2,3},{3,2},{4,5},{5,4},{6,7},{7,6},{8,9},{9,8},{10,11... | collective-permute-start | bytes 2359304 | tf_op jit(solution)/shard_map/ppermute | solution.py:323
  133.0 123.3 %slice-start.1 = ((s8[4718592]{0:T(1024)(128)(4,1)}), s8[524288]{0:T(1024)(128)(4,1)S(1)}, s32[]{:S(2)}) async-start(s8[4718592]{0:T(1024)(128)(4,1)} %bitcast.10), calls=%async_computation.4 | async-start | bytes 1048576
  153.9 102.5 %copy-start = (bf16[1,128,1536]{2,1,0:T(8,128)(2,1)S(1)}, bf16[1,128,1536]{2,1,0:T(8,128)(2,1)}, u32[]{:S(2)}) copy-start(bf16[1,128,1536]{2,1,0:T(8,128)(2,1)} %param.9) | copy-start | bytes 1179652
  153.9 102.5 %copy-start.1 = (f32[1,1536]{1,0:T(1,128)S(1)}, f32[1,1536]{1,0:T(1,128)}, u32[]{:S(2)}) copy-start(f32[1,1536]{1,0:T(1,128)} %gate_ref.1) | copy-start | bytes 18436

commit v2 on v1

--- a/solution.py
+++ b/solution.py
@@ -164,8 +164,10 @@
         lax.fori_loop(0, count, lambda head, carry: (step(head), carry)[1], 0)
 
 
-def cross_kernel(count, has_before, has_token, q_ref, *refs):
+def cross_kernel(count, has_before, has_token, handed, q_ref, *refs):
     rows, out_ref = refs[:count], refs[-1]
+    if handed:
+        refs[-2][...] = rows[-1][...]
     if has_token:
         refs[-2][...] = jnp.zeros((8, 128), jnp.float32)
     each_head(3, lambda head: cross_head(head, q_ref, rows, out_ref))
@@ -259,11 +261,12 @@
     each_head(3, whole)
 
 
-def cross_attend(q, rows, before=None, wait=None, token=False):
+def cross_attend(q, rows, before=None, wait=None, token=False, hand_on=False):
     others = [array for array in (before, wait) if array is not None]
     return pl.pallas_call(
-        functools.partial(cross_kernel, len(rows), before is not None, token),
+        functools.partial(cross_kernel, len(rows), before is not None, token, hand_on),
         out_shape=[jax.ShapeDtypeStruct((8, 128), jnp.float32)] * token
+        + [jax.ShapeDtypeStruct(rows[-1].shape, jnp.bfloat16)] * hand_on
         + [jax.ShapeDtypeStruct((3, 80, 1024), jnp.float32)],
         compiler_params=PARAMS,
         name="cross",
@@ -336,8 +339,8 @@
     kv_x = shifted(kv, "xl", 2, 1)
     column = [kv, shifted(kv, "core", 2, 1), kv_x, shifted(kv_x, "core", 2, 1)]
     q_far = shifted(q, "core", 2, 1)
-    token, near = cross_attend(q, [row, back, ahead], token=True)
-    (far,) = cross_attend(q_far, [row, back, ahead], wait=token)
+    ahead, near = cross_attend(q, [row, back, ahead], hand_on=True)
+    (far,) = cross_attend(q_far, [row, back, ahead])
     token, far = cross_attend(q_far, [across], before=far, token=True)
     far = shifted(far, "core", 2, 1)
     (near,) = cross_attend(q, [across], before=near, wait=token)

time: 258 us -> 257 us (level)
  no operation moved by 1% of the time
where the time goes in v2:
time: 257 us
  Pallas kernels  184 us (72%)
  blocking collectives  37.4 us (15%)
  waiting for transfers between devices  21.1 us (8%)
  starting transfers between devices  14.3 us (6%)
    pallas_call x4, Pallas kernels, cross_attend(): pl.pallas_call(functools.partial(cross_kernel, len(rows), before is not N...  95.1 us
    pallas_call x1, Pallas kernels, own_attend(): pl.pallas_call(own_kernel, out_shape=jax.ShapeDtypeStruct((8, 3, 64, 128)...  83.9 us
    ppermute x11, waiting for transfers between devices, shifted(): lax.ppermute(array, axis, [(i, (i + step) % size) for i in range(size)])  21.1 us
    all_to_all x1, blocking collectives, body(): pool = lax.all_to_all(pool, 'z', 0, 0, tiled=True)  18.9 us
    all_to_all x1, blocking collectives, body(): returned = lax.all_to_all(heads, 'z', 0, 0, tiled=True)  18.5 us
    ppermute x11, starting transfers between devices, shifted(): lax.ppermute(array, axis, [(i, (i + step) % size) for i in range(size)])  10.7 us
  transfers between devices with their start and end apart: 12, of which 4 were waited for; matrix products, arithmetic and copies ran while one was open for 0% of the time, Pallas kernels for 37%

profile of v2, /device:TPU:2, one launch (start us, length us, event | category | flops | bytes accessed | tf_op | source)
XLA Modules:
  0.0 256.7 jit_solution(592080887212595662)
XLA Ops:
  0.0 2.8 %prep.1 = (bf16[8,2,3,16,128]{4,3,2,1,0:T(8,128)(2,1)}, bf16[8,3,192,128]{3,2,1,0:T(8,128)(2,1)}) custom-call(bf16[128,1536]{1,0:T(8,128)(2,1)} %bitcast.15, bf16[128,1536]{1,0:T(8,128)(2,1)} %bitcast.16, bf16[128,1536]{1,0:T(8,128)(2,1)} %bitcast.17), custom_call_target="tpu_custom_call" | custom-call | tf_op jit(solution)/shard_map/prep/pallas_call | solution.py:58
  2.8 18.9 %all_to_all.15.pool_ref = bf16[8,2,3,16,128]{4,3,2,1,0:T(8,128)(2,1)S(1)} all-to-all(bf16[8,2,3,16,128]{4,3,2,1,0:T(8,128)(2,1)} %get-tuple-element.16), channel_id=1, replica_groups=mesh['y'=4,'xh'=2,'xl'=2,'z'=8,'core'=2] {'z'}, dimensions={0} | all-to-all | bytes 393216 | tf_op jit(solution)/shard_map/all_to_all | solution.py:332
  21.8 3.6 %all-to-all-start = ((bf16[8,3,192,128]{3,2,1,0:T(8,128)(2,1)}), bf16[8,3,192,128]{3,2,1,0:T(8,128)(2,1)S(1)}, u32[]{:S(2)}, u32[]{:S(2)}) async-start(bf16[8,3,192,128]{3,2,1,0:T(8,128)(2,1)} %get-tuple-element.13), calls=%async_computation | async-start | bytes 2359296 | tf_op jit(solution)/shard_map/all_to_all | solution.py:333
  25.4 0.1 repack.1
  25.4 1.6 collective-permute-start.3
  27.0 0.5 collective-permute-start.4
  27.5 2.1 collective-permute-start.5
  29.7 3.5 %collective-permute-done.3 = bf16[2,3,128,128]{3,2,1,0:T(8,128)(2,1)S(1)} collective-permute-done((bf16[2,3,128,128]{3,2,1,0:T(8,128)(2,1)S(1)}, bf16[2,3,128,128]{3,2,1,0:T(8,128)(2,1)S(1)}, u32[]{:S(2)}, u32[]{:S(2)}) %collective-permute-start.3) | collective-permute-done | bytes 196640 | tf_op jit(solution)/shard_map/ppermute | solution.py:326
  33.2 1.0 collective-permute-done.4
  34.2 2.1 collective-permute-done.5
  36.3 0.1 pad_maximum_fusion.refs_0_
  36.4 1.7 collective-permute-start.6
  38.0 1.7 collective-permute-start.8
  39.7 14.5 %collective-permute-done.6.refs_1_ = bf16[2,4,3,128,128]{4,3,2,1,0:T(8,128)(2,1)S(1)} collective-permute-done((bf16[2,4,3,128,128]{4,3,2,1,0:T(8,128)(2,1)S(1)}, bf16[2,4,3,128,128]{4,3,2,1,0:T(8,128)(2,1)S(1)}, u32[]{:S(2)}, u32[]{:S(2)}) %collective-permute-start.6) | collective-permute-done | bytes 786464 | tf_op jit(solution)/shard_map/ppermute | solution.py:326
  54.2 1.5 collective-permute-start.7
  55.6 0.0 all-to-all-done.own_ref
  55.6 0.1 split.1
  55.7 1.0 collective-permute-start.1
  56.7 0.0 collective-permute-start.9
  56.7 0.0 collective-permute-done.8.refs_2_
  56.7 62.1 %cross.4 = (bf16[2,4,3,128,128]{4,3,2,1,0:T(8,128)(2,1)S(1)}, f32[3,80,1024]{2,1,0:T(8,128)S(1)}) custom-call(bf16[8,3,64,128]{3,2,1,0:T(8,128)(2,1)S(1)} %get-tuple-element.14.q_ref, bf16[2,4,3,128,128]{4,3,2,1,0:T(8,128)(2,1)S(1)} %pad_maximum_fusion.refs_0_, bf16[2,4,3,128,128]{4,3,2,1,0:T(8,128)(2,1)S(1)} %collective-permute-done.6.refs_1_, ...), custom_call_target="tpu_custom_call" | custom-call | tf_op jit(solution)/shard_map/cross/pallas_call | solution.py:266
  118.8 0.0 collective-permute-done.9.q_ref
  118.9 0.0 slice-start
  118.9 8.8 %cross.5.refs_1_ = f32[3,80,1024]{2,1,0:T(8,128)S(1)} custom-call(bf16[8,3,64,128]{3,2,1,0:T(8,128)(2,1)S(1)} %collective-permute-done.9.q_ref, bf16[2,4,3,128,128]{4,3,2,1,0:T(8,128)(2,1)S(1)} %pad_maximum_fusion.refs_0_, bf16[2,4,3,128,128]{4,3,2,1,0:T(8,128)(2,1)S(1)} %collective-permute-done.6.refs_1_, ...), custom_call_target="tpu_custom_call" | custom-call | tf_op jit(solution)/shard_map/cross/pallas_call | solution.py:266
  127.6 0.0 collective-permute-done.7.refs_0_
  127.7 3.4 %cross.6 = (f32[8,128]{1,0:T(8,128)S(1)}, f32[3,80,1024]{2,1,0:T(8,128)S(1)}) custom-call(bf16[8,3,64,128]{3,2,1,0:T(8,128)(2,1)S(1)} %collective-permute-done.9.q_ref, bf16[2,4,3,128,128]{4,3,2,1,0:T(8,128)(2,1)S(1)} %collective-permute-done.7.refs_0_, f32[3,80,1024]{2,1,0:T(8,128)S(1)} %cross.5.refs_1_), custom_call_target="tpu_custom_call" | custom-call | tf_op jit(solution)/shard_map/cross/pallas_call | solution.py:266
  131.0 0.1 collective-permute-start.10
  131.1 0.5 collective-permute-start
  131.6 0.0 collective-permute-done.1.kv2
  131.6 0.1 collective-permute-start.2
  131.7 0.0 slice-start.1
  131.7 20.9 %cross.7.near_ref = f32[3,80,1024]{2,1,0:T(8,128)S(1)} custom-call(bf16[8,3,64,128]{3,2,1,0:T(8,128)(2,1)S(1)} %get-tuple-element.14.q_ref, bf16[2,4,3,128,128]{4,3,2,1,0:T(8,128)(2,1)S(1)} %collective-permute-done.7.refs_0_, f32[3,80,1024]{2,1,0:T(8,128)S(1)} %get-tuple-element.17.refs_1_, f32[8,128]{1,0:T(8,128)S(1)} %get-tuple-element.19.refs_2_), custom_call_target="tpu_custom_call" | custom-call | tf_op jit(solution)/shard_map/cross/pallas_call | solution.py:266
  152.6 0.0 copy-start
  152.6 0.0 copy-start.1
  152.6 0.0 collective-permute-done.kv1
  152.7 0.0 collective-permute-done.10.far_ref
  152.7 0.0 collective-permute-done.2.kv3
  152.7 83.9 %own.1 = bf16[8,3,64,128]{3,2,1,0:T(8,128)(2,1)S(1)} custom-call(bf16[8,3,64,128]{3,2,1,0:T(8,128)(2,1)S(1)} %get-tuple-element.14.q_ref, bf16[8,3,128,128]{3,2,1,0:T(8,128)(2,1)S(1)} %get-tuple-element.15.kv0, bf16[8,3,128,128]{3,2,1,0:T(8,128)(2,1)S(1)} %collective-permute-done.kv1, bf16[8,3,128,128]{3,2,1,0:T(8,128)(2,1)S(1)} %collective-permute-done.1.kv2, ...), custom_call_target="tpu_custom_call" | custom-call | tf_op jit(solution)/shard_map/own/pallas_call | solution.py:294
  236.6 18.5 %all_to_all.16 = bf16[8,3,64,128]{3,2,1,0:T(8,128)(2,1)S(1)} all-to-all(bf16[8,3,64,128]{3,2,1,0:T(8,128)(2,1)S(1)} %own.1), channel_id=1, replica_groups=mesh['y'=4,'xh'=2,'xl'=2,'z'=8,'core'=2] {'z'}, dimensions={0} | all-to-all | bytes 786432 | tf_op jit(solution)/shard_map/all_to_all | solution.py:348
  255.1 0.0 slice-done
  255.1 0.0 slice-done.1
  255.1 0.0 copy-done
  255.1 0.0 copy-done.1
  255.1 1.6 project.1
  (1 shorter events, 0.0 us)
Async XLA Ops:
  21.8 33.9 %all-to-all-start = ((bf16[8,3,192,128]{3,2,1,0:T(8,128)(2,1)}), bf16[8,3,192,128]{3,2,1,0:T(8,128)(2,1)S(1)}, u32[]{:S(2)}, u32[]{:S(2)}) async-start(bf16[8,3,192,128]{3,2,1,0:T(8,128)(2,1)} %get-tuple-element.13), calls=%async_computation | async-start | bytes 2359296 | tf_op jit(solution)/shard_map/all_to_all | solution.py:333
  25.4 7.8 %collective-permute-start.3 = (bf16[2,3,128,128]{3,2,1,0:T(8,128)(2,1)S(1)}, bf16[2,3,128,128]{3,2,1,0:T(8,128)(2,1)S(1)}, u32[]{:S(2)}, u32[]{:S(2)}) collective-permute-start(bf16[2,3,128,128]{3,2,1,0:T(8,128)(2,1)S(1)} %repack.1), channel_id=1, source_target_pairs={{0,16},{16,32},{32,48},{48,0},{1,17},{17,33},{33,49},{49,1},{2,18}... | collective-permute-start | bytes 589832 | tf_op jit(solution)/shard_map/ppermute | solution.py:326
  27.0 7.2 %collective-permute-start.4 = (bf16[2,3,128,128]{3,2,1,0:T(8,128)(2,1)S(1)}, bf16[2,3,128,128]{3,2,1,0:T(8,128)(2,1)S(1)}, u32[]{:S(2)}, u32[]{:S(2)}) collective-permute-start(bf16[2,3,128,128]{3,2,1,0:T(8,128)(2,1)S(1)} %repack.1), channel_id=1, source_target_pairs={{0,48},{16,0},{32,16},{48,32},{1,49},{17,1},{33,17},{49,33},{2,50}... | collective-permute-start | bytes 589832 | tf_op jit(solution)/shard_map/ppermute | solution.py:326
  27.5 8.7 %collective-permute-start.5 = (bf16[2,3,128,128]{3,2,1,0:T(8,128)(2,1)S(1)}, bf16[2,3,128,128]{3,2,1,0:T(8,128)(2,1)S(1)}, u32[]{:S(2)}, u32[]{:S(2)}) collective-permute-start(bf16[2,3,128,128]{3,2,1,0:T(8,128)(2,1)S(1)} %repack.1), channel_id=1, source_target_pairs={{0,32},{16,48},{32,0},{48,16},{1,33},{17,49},{33,1},{49,17},{2,34}... | collective-permute-start | bytes 589832 | tf_op jit(solution)/shard_map/ppermute | solution.py:326
  36.4 17.8 %collective-permute-start.6 = (bf16[2,4,3,128,128]{4,3,2,1,0:T(8,128)(2,1)S(1)}, bf16[2,4,3,128,128]{4,3,2,1,0:T(8,128)(2,1)S(1)}, u32[]{:S(2)}, u32[]{:S(2)}) collective-permute-start(bf16[2,4,3,128,128]{4,3,2,1,0:T(8,128)(2,1)S(1)} %pad_maximum_fusion.refs_0_), channel_id=1, source_target_pairs={{0,64},{64,128},{128,192},{192,0},{1,65},{65,129},{129,193},{193,1... | collective-permute-start | bytes 2359304 | tf_op jit(solution)/shard_map/ppermute | solution.py:326
  38.0 18.7 %collective-permute-start.8 = (bf16[2,4,3,128,128]{4,3,2,1,0:T(8,128)(2,1)S(1)}, bf16[2,4,3,128,128]{4,3,2,1,0:T(8,128)(2,1)}, u32[]{:S(2)}, u32[]{:S(2)}) collective-permute-start(bf16[2,4,3,128,128]{4,3,2,1,0:T(8,128)(2,1)S(1)} %pad_maximum_fusion.refs_0_), channel_id=1, source_target_pairs={{0,192},{64,0},{128,64},{192,128},{1,193},{65,1},{129,65},{193,129... | collective-permute-start | bytes 2359304 | tf_op jit(solution)/shard_map/ppermute | solution.py:326
  54.2 73.5 %collective-permute-start.7 = (bf16[2,4,3,128,128]{4,3,2,1,0:T(8,128)(2,1)S(1)}, bf16[2,4,3,128,128]{4,3,2,1,0:T(8,128)(2,1)S(1)}, u32[]{:S(2)}, u32[]{:S(2)}) collective-permute-start(bf16[2,4,3,128,128]{4,3,2,1,0:T(8,128)(2,1)S(1)} %collective-permute-done.6.refs_1_), channel_id=1, source_target_pairs={{0,64},{64,128},{128,192},{192,0},{1,65},{65,129},{129,193},{193,1... | collective-permute-start | bytes 2359304 | tf_op jit(solution)/shard_map/ppermute | solution.py:326
  55.7 75.9 %collective-permute-start.1 = (bf16[8,3,128,128]{3,2,1,0:T(8,128)(2,1)S(1)}, bf16[8,3,128,128]{3,2,1,0:T(8,128)(2,1)S(1)}, u32[]{:S(2)}, u32[]{:S(2)}) collective-permute-start(bf16[8,3,128,128]{3,2,1,0:T(8,128)(2,1)S(1)} %get-tuple-element.15.kv0), channel_id=1, source_target_pairs={{0,16},{16,0},{1,17},{17,1},{2,18},{18,2},{3,19},{19,3},{4,20},{20... | collective-permute-start | bytes 2359304 | tf_op jit(solution)/shard_map/ppermute | solution.py:326
  56.7 62.1 %collective-permute-start.9 = (bf16[8,3,64,128]{3,2,1,0:T(8,128)(2,1)S(1)}, bf16[8,3,64,128]{3,2,1,0:T(8,128)(2,1)S(1)}, u32[]{:S(2)}, u32[]{:S(2)}) collective-permute-start(bf16[8,3,64,128]{3,2,1,0:T(8,128)(2,1)S(1)} %get-tuple-element.14.q_ref), channel_id=1, source_target_pairs={{0,1},{1,0},{2,3},{3,2},{4,5},{5,4},{6,7},{7,6},{8,9},{9,8},{10,11... | collective-permute-start | bytes 1179656 | tf_op jit(solution)/shard_map/ppermute | solution.py:326
  118.9 136.2 %slice-start = ((s8[4718592]{0:T(1024)(128)(4,1)}), s8[4194304]{0:T(1024)(128)(4,1)S(1)}, s32[]{:S(2)}) async-start(s8[4718592]{0:T(1024)(128)(4,1)} %bitcast.10), calls=%async_computation.3 | async-start | bytes 8388608
  131.0 21.6 %collective-permute-start.10 = (f32[3,80,1024]{2,1,0:T(8,128)S(1)}, f32[3,80,1024]{2,1,0:T(8,128)S(1)}, u32[]{:S(2)}, u32[]{:S(2)}) collective-permute-start(f32[3,80,1024]{2,1,0:T(8,128)S(1)} %get-tuple-element.20), channel_id=1, source_target_pairs={{0,1},{1,0},{2,3},{3,2},{4,5},{5,4},{6,7},{7,6},{8,9},{9,8},{10,11... | collective-permute-start | bytes 2949128 | tf_op jit(solution)/shard_map/ppermute | solution.py:326
  131.1 21.5 %collective-permute-start = (bf16[8,3,128,128]{3,2,1,0:T(8,128)(2,1)S(1)}, bf16[8,3,128,128]{3,2,1,0:T(8,128)(2,1)S(1)}, u32[]{:S(2)}, u32[]{:S(2)}) collective-permute-start(bf16[8,3,128,128]{3,2,1,0:T(8,128)(2,1)S(1)} %get-tuple-element.15.kv0), channel_id=1, source_target_pairs={{0,1},{1,0},{2,3},{3,2},{4,5},{5,4},{6,7},{7,6},{8,9},{9,8},{10,11... | collective-permute-start | bytes 2359304 | tf_op jit(solution)/shard_map/ppermute | solution.py:326
  131.6 21.0 %collective-permute-start.2 = (bf16[8,3,128,128]{3,2,1,0:T(8,128)(2,1)S(1)}, bf16[8,3,128,128]{3,2,1,0:T(8,128)(2,1)S(1)}, u32[]{:S(2)}, u32[]{:S(2)}) collective-permute-start(bf16[8,3,128,128]{3,2,1,0:T(8,128)(2,1)S(1)} %collective-permute-done.1.kv2), channel_id=1, source_target_pairs={{0,1},{1,0},{2,3},{3,2},{4,5},{5,4},{6,7},{7,6},{8,9},{9,8},{10,11... | collective-permute-start | bytes 2359304 | tf_op jit(solution)/shard_map/ppermute | solution.py:326
  131.7 123.4 %slice-start.1 = ((s8[4718592]{0:T(1024)(128)(4,1)}), s8[524288]{0:T(1024)(128)(4,1)S(1)}, s32[]{:S(2)}) async-start(s8[4718592]{0:T(1024)(128)(4,1)} %bitcast.10), calls=%async_computation.4 | async-start | bytes 1048576
  152.6 102.5 %copy-start = (bf16[1,128,1536]{2,1,0:T(8,128)(2,1)S(1)}, bf16[1,128,1536]{2,1,0:T(8,128)(2,1)}, u32[]{:S(2)}) copy-start(bf16[1,128,1536]{2,1,0:T(8,128)(2,1)} %param.9) | copy-start | bytes 1179652
  152.6 102.5 %copy-start.1 = (f32[1,1536]{1,0:T(1,128)S(1)}, f32[1,1536]{1,0:T(1,128)}, u32[]{:S(2)}) copy-start(f32[1,1536]{1,0:T(1,128)} %gate_ref.1) | copy-start | bytes 18436

commit v3 on v2

--- a/solution.py
+++ b/solution.py
@@ -249,16 +249,20 @@
     kvs = (kv0, kv1, kv2, kv3)
     rest = kvs, near_ref, far_ref, out_ref, p_ref
 
-    def whole(head):
-        sum_ref[head, 0:1] = own_weights(head, q_ref, kvs, p_ref)
-
-        @pl.when(outside(sum_ref[head, 0:1]))
-        def _():
+    def plain(head):
+        sums = own_weights(head, q_ref, kvs, p_ref)
+        sum_ref[head, 0:1] = sums
+        own_finish(head, *rest, sums)
+
+    each_head(3, plain)
+
+    @pl.when(outside(sum_ref[:, 0:1]))
+    def _():
+        def again(head):
             own_shifted(head, q_ref, kvs, p_ref, sum_ref)
-
-        own_finish(head, *rest, sum_ref[head, 0:1])
-
-    each_head(3, whole)
+            own_finish(head, *rest, sum_ref[head, 0:1])
+
+        each_head(3, again)
 
 
 def cross_attend(q, rows, before=None, wait=None, token=False, hand_on=False):

time: 257 us -> 261 us (1.016)
  Pallas kernels: 184 us -> 188 us
    pallas_call x1, Pallas kernels: 83.9 us -> 88.3 us  [own_attend(): pl.pallas_call(own_kernel, out_shape=jax.ShapeDtypeStruct((8, 3, 64, 128)...]
  transfers between devices with their start and end apart: 12 -> 12, of which waited for: 4 -> 4; matrix products, arithmetic and copies ran while one was open for 0% -> 0% of each run, Pallas kernels for 37% -> 36%
where the time goes in v3:
time: 261 us
  Pallas kernels  188 us (72%)
  blocking collectives  37.4 us (14%)
  waiting for transfers between devices  21.1 us (8%)
  starting transfers between devices  14.3 us (5%)
    pallas_call x4, Pallas kernels, cross_attend(): pl.pallas_call(functools.partial(cross_kernel, len(rows), before is not N...  95.1 us
    pallas_call x1, Pallas kernels, own_attend(): pl.pallas_call(own_kernel, out_shape=jax.ShapeDtypeStruct((8, 3, 64, 128)...  88.3 us
    ppermute x11, waiting for transfers between devices, shifted(): lax.ppermute(array, axis, [(i, (i + step) % size) for i in range(size)])  21.1 us
    all_to_all x1, blocking collectives, body(): pool = lax.all_to_all(pool, 'z', 0, 0, tiled=True)  18.9 us
    all_to_all x1, blocking collectives, body(): returned = lax.all_to_all(heads, 'z', 0, 0, tiled=True)  18.5 us
    ppermute x11, starting transfers between devices, shifted(): lax.ppermute(array, axis, [(i, (i + step) % size) for i in range(size)])  10.7 us
  transfers between devices with their start and end apart: 12, of which 4 were waited for; matrix products, arithmetic and copies ran while one was open for 0% of the time, Pallas kernels for 36%

profile of v3, /device:TPU:2, one launch (start us, length us, event | category | flops | bytes accessed | tf_op | source)
XLA Modules:
  0.0 261.1 jit_solution(13548758013746365319)
XLA Ops:
  0.0 2.8 %prep.1 = (bf16[8,2,3,16,128]{4,3,2,1,0:T(8,128)(2,1)}, bf16[8,3,192,128]{3,2,1,0:T(8,128)(2,1)}) custom-call(bf16[128,1536]{1,0:T(8,128)(2,1)} %bitcast.15, bf16[128,1536]{1,0:T(8,128)(2,1)} %bitcast.16, bf16[128,1536]{1,0:T(8,128)(2,1)} %bitcast.17), custom_call_target="tpu_custom_call" | custom-call | tf_op jit(solution)/shard_map/prep/pallas_call | solution.py:58
  2.8 18.9 %all_to_all.15.pool_ref = bf16[8,2,3,16,128]{4,3,2,1,0:T(8,128)(2,1)S(1)} all-to-all(bf16[8,2,3,16,128]{4,3,2,1,0:T(8,128)(2,1)} %get-tuple-element.16), channel_id=1, replica_groups=mesh['y'=4,'xh'=2,'xl'=2,'z'=8,'core'=2] {'z'}, dimensions={0} | all-to-all | bytes 393216 | tf_op jit(solution)/shard_map/all_to_all | solution.py:336
  21.8 3.6 %all-to-all-start = ((bf16[8,3,192,128]{3,2,1,0:T(8,128)(2,1)}), bf16[8,3,192,128]{3,2,1,0:T(8,128)(2,1)S(1)}, u32[]{:S(2)}, u32[]{:S(2)}) async-start(bf16[8,3,192,128]{3,2,1,0:T(8,128)(2,1)} %get-tuple-element.13), calls=%async_computation | async-start | bytes 2359296 | tf_op jit(solution)/shard_map/all_to_all | solution.py:337
  25.4 0.1 repack.1
  25.4 1.6 collective-permute-start.3
  27.0 0.5 collective-permute-start.4
  27.5 2.1 collective-permute-start.5
  29.7 3.5 %collective-permute-done.3 = bf16[2,3,128,128]{3,2,1,0:T(8,128)(2,1)S(1)} collective-permute-done((bf16[2,3,128,128]{3,2,1,0:T(8,128)(2,1)S(1)}, bf16[2,3,128,128]{3,2,1,0:T(8,128)(2,1)S(1)}, u32[]{:S(2)}, u32[]{:S(2)}) %collective-permute-start.3) | collective-permute-done | bytes 196640 | tf_op jit(solution)/shard_map/ppermute | solution.py:330
  33.2 1.0 collective-permute-done.4
  34.2 2.1 collective-permute-done.5
  36.3 0.1 pad_maximum_fusion.refs_0_
  36.4 1.7 collective-permute-start.6
  38.0 1.7 collective-permute-start.8
  39.7 14.5 %collective-permute-done.6.refs_1_ = bf16[2,4,3,128,128]{4,3,2,1,0:T(8,128)(2,1)S(1)} collective-permute-done((bf16[2,4,3,128,128]{4,3,2,1,0:T(8,128)(2,1)S(1)}, bf16[2,4,3,128,128]{4,3,2,1,0:T(8,128)(2,1)S(1)}, u32[]{:S(2)}, u32[]{:S(2)}) %collective-permute-start.6) | collective-permute-done | bytes 786464 | tf_op jit(solution)/shard_map/ppermute | solution.py:330
  54.2 1.5 collective-permute-start.7
  55.6 0.0 all-to-all-done.own_ref
  55.6 0.1 split.1
  55.7 1.0 collective-permute-start.1
  56.7 0.0 collective-permute-start.9
  56.7 0.0 collective-permute-done.8.refs_2_
  56.7 62.1 %cross.4 = (bf16[2,4,3,128,128]{4,3,2,1,0:T(8,128)(2,1)S(1)}, f32[3,80,1024]{2,1,0:T(8,128)S(1)}) custom-call(bf16[8,3,64,128]{3,2,1,0:T(8,128)(2,1)S(1)} %get-tuple-element.14.q_ref, bf16[2,4,3,128,128]{4,3,2,1,0:T(8,128)(2,1)S(1)} %pad_maximum_fusion.refs_0_, bf16[2,4,3,128,128]{4,3,2,1,0:T(8,128)(2,1)S(1)} %collective-permute-done.6.refs_1_, ...), custom_call_target="tpu_custom_call" | custom-call | tf_op jit(solution)/shard_map/cross/pallas_call | solution.py:270
  118.8 0.0 collective-permute-done.9.q_ref
  118.9 0.0 slice-start
  118.9 8.8 %cross.5.refs_1_ = f32[3,80,1024]{2,1,0:T(8,128)S(1)} custom-call(bf16[8,3,64,128]{3,2,1,0:T(8,128)(2,1)S(1)} %collective-permute-done.9.q_ref, bf16[2,4,3,128,128]{4,3,2,1,0:T(8,128)(2,1)S(1)} %pad_maximum_fusion.refs_0_, bf16[2,4,3,128,128]{4,3,2,1,0:T(8,128)(2,1)S(1)} %collective-permute-done.6.refs_1_, ...), custom_call_target="tpu_custom_call" | custom-call | tf_op jit(solution)/shard_map/cross/pallas_call | solution.py:270
  127.6 0.0 collective-permute-done.7.refs_0_
  127.7 3.4 %cross.6 = (f32[8,128]{1,0:T(8,128)S(1)}, f32[3,80,1024]{2,1,0:T(8,128)S(1)}) custom-call(bf16[8,3,64,128]{3,2,1,0:T(8,128)(2,1)S(1)} %collective-permute-done.9.q_ref, bf16[2,4,3,128,128]{4,3,2,1,0:T(8,128)(2,1)S(1)} %collective-permute-done.7.refs_0_, f32[3,80,1024]{2,1,0:T(8,128)S(1)} %cross.5.refs_1_), custom_call_target="tpu_custom_call" | custom-call | tf_op jit(solution)/shard_map/cross/pallas_call | solution.py:270
  131.0 0.1 collective-permute-start.10
  131.1 0.5 collective-permute-start
  131.6 0.0 collective-permute-done.1.kv2
  131.6 0.1 collective-permute-start.2
  131.7 0.0 slice-start.1
  131.7 20.9 %cross.7.near_ref = f32[3,80,1024]{2,1,0:T(8,128)S(1)} custom-call(bf16[8,3,64,128]{3,2,1,0:T(8,128)(2,1)S(1)} %get-tuple-element.14.q_ref, bf16[2,4,3,128,128]{4,3,2,1,0:T(8,128)(2,1)S(1)} %collective-permute-done.7.refs_0_, f32[3,80,1024]{2,1,0:T(8,128)S(1)} %get-tuple-element.17.refs_1_, f32[8,128]{1,0:T(8,128)S(1)} %get-tuple-element.19.refs_2_), custom_call_target="tpu_custom_call" | custom-call | tf_op jit(solution)/shard_map/cross/pallas_call | solution.py:270
  152.6 0.0 copy-start
  152.6 0.0 copy-start.1
  152.6 0.0 collective-permute-done.kv1
  152.7 0.0 collective-permute-done.10.far_ref
  152.7 0.0 collective-permute-done.2.kv3
  152.7 88.3 %own.1 = bf16[8,3,64,128]{3,2,1,0:T(8,128)(2,1)S(1)} custom-call(bf16[8,3,64,128]{3,2,1,0:T(8,128)(2,1)S(1)} %get-tuple-element.14.q_ref, bf16[8,3,128,128]{3,2,1,0:T(8,128)(2,1)S(1)} %get-tuple-element.15.kv0, bf16[8,3,128,128]{3,2,1,0:T(8,128)(2,1)S(1)} %collective-permute-done.kv1, bf16[8,3,128,128]{3,2,1,0:T(8,128)(2,1)S(1)} %collective-permute-done.1.kv2, ...), custom_call_target="tpu_custom_call" | custom-call | tf_op jit(solution)/shard_map/own/pallas_call | solution.py:298
  241.0 18.5 %all_to_all.16 = bf16[8,3,64,128]{3,2,1,0:T(8,128)(2,1)S(1)} all-to-all(bf16[8,3,64,128]{3,2,1,0:T(8,128)(2,1)S(1)} %own.1), channel_id=1, replica_groups=mesh['y'=4,'xh'=2,'xl'=2,'z'=8,'core'=2] {'z'}, dimensions={0} | all-to-all | bytes 786432 | tf_op jit(solution)/shard_map/all_to_all | solution.py:352
  259.5 0.0 slice-done
  259.5 0.0 slice-done.1
  259.5 0.0 copy-done
  259.6 0.0 copy-done.1
  259.6 1.6 project.1
  (1 shorter events, 0.0 us)
Async XLA Ops:
  21.8 33.9 %all-to-all-start = ((bf16[8,3,192,128]{3,2,1,0:T(8,128)(2,1)}), bf16[8,3,192,128]{3,2,1,0:T(8,128)(2,1)S(1)}, u32[]{:S(2)}, u32[]{:S(2)}) async-start(bf16[8,3,192,128]{3,2,1,0:T(8,128)(2,1)} %get-tuple-element.13), calls=%async_computation | async-start | bytes 2359296 | tf_op jit(solution)/shard_map/all_to_all | solution.py:337
  25.4 7.8 %collective-permute-start.3 = (bf16[2,3,128,128]{3,2,1,0:T(8,128)(2,1)S(1)}, bf16[2,3,128,128]{3,2,1,0:T(8,128)(2,1)S(1)}, u32[]{:S(2)}, u32[]{:S(2)}) collective-permute-start(bf16[2,3,128,128]{3,2,1,0:T(8,128)(2,1)S(1)} %repack.1), channel_id=1, source_target_pairs={{0,16},{16,32},{32,48},{48,0},{1,17},{17,33},{33,49},{49,1},{2,18}... | collective-permute-start | bytes 589832 | tf_op jit(solution)/shard_map/ppermute | solution.py:330
  27.0 7.2 %collective-permute-start.4 = (bf16[2,3,128,128]{3,2,1,0:T(8,128)(2,1)S(1)}, bf16[2,3,128,128]{3,2,1,0:T(8,128)(2,1)S(1)}, u32[]{:S(2)}, u32[]{:S(2)}) collective-permute-start(bf16[2,3,128,128]{3,2,1,0:T(8,128)(2,1)S(1)} %repack.1), channel_id=1, source_target_pairs={{0,48},{16,0},{32,16},{48,32},{1,49},{17,1},{33,17},{49,33},{2,50}... | collective-permute-start | bytes 589832 | tf_op jit(solution)/shard_map/ppermute | solution.py:330
  27.5 8.7 %collective-permute-start.5 = (bf16[2,3,128,128]{3,2,1,0:T(8,128)(2,1)S(1)}, bf16[2,3,128,128]{3,2,1,0:T(8,128)(2,1)S(1)}, u32[]{:S(2)}, u32[]{:S(2)}) collective-permute-start(bf16[2,3,128,128]{3,2,1,0:T(8,128)(2,1)S(1)} %repack.1), channel_id=1, source_target_pairs={{0,32},{16,48},{32,0},{48,16},{1,33},{17,49},{33,1},{49,17},{2,34}... | collective-permute-start | bytes 589832 | tf_op jit(solution)/shard_map/ppermute | solution.py:330
  36.4 17.8 %collective-permute-start.6 = (bf16[2,4,3,128,128]{4,3,2,1,0:T(8,128)(2,1)S(1)}, bf16[2,4,3,128,128]{4,3,2,1,0:T(8,128)(2,1)S(1)}, u32[]{:S(2)}, u32[]{:S(2)}) collective-permute-start(bf16[2,4,3,128,128]{4,3,2,1,0:T(8,128)(2,1)S(1)} %pad_maximum_fusion.refs_0_), channel_id=1, source_target_pairs={{0,64},{64,128},{128,192},{192,0},{1,65},{65,129},{129,193},{193,1... | collective-permute-start | bytes 2359304 | tf_op jit(solution)/shard_map/ppermute | solution.py:330
  38.0 18.7 %collective-permute-start.8 = (bf16[2,4,3,128,128]{4,3,2,1,0:T(8,128)(2,1)S(1)}, bf16[2,4,3,128,128]{4,3,2,1,0:T(8,128)(2,1)}, u32[]{:S(2)}, u32[]{:S(2)}) collective-permute-start(bf16[2,4,3,128,128]{4,3,2,1,0:T(8,128)(2,1)S(1)} %pad_maximum_fusion.refs_0_), channel_id=1, source_target_pairs={{0,192},{64,0},{128,64},{192,128},{1,193},{65,1},{129,65},{193,129... | collective-permute-start | bytes 2359304 | tf_op jit(solution)/shard_map/ppermute | solution.py:330
  54.2 73.5 %collective-permute-start.7 = (bf16[2,4,3,128,128]{4,3,2,1,0:T(8,128)(2,1)S(1)}, bf16[2,4,3,128,128]{4,3,2,1,0:T(8,128)(2,1)S(1)}, u32[]{:S(2)}, u32[]{:S(2)}) collective-permute-start(bf16[2,4,3,128,128]{4,3,2,1,0:T(8,128)(2,1)S(1)} %collective-permute-done.6.refs_1_), channel_id=1, source_target_pairs={{0,64},{64,128},{128,192},{192,0},{1,65},{65,129},{129,193},{193,1... | collective-permute-start | bytes 2359304 | tf_op jit(solution)/shard_map/ppermute | solution.py:330
  55.7 75.9 %collective-permute-start.1 = (bf16[8,3,128,128]{3,2,1,0:T(8,128)(2,1)S(1)}, bf16[8,3,128,128]{3,2,1,0:T(8,128)(2,1)S(1)}, u32[]{:S(2)}, u32[]{:S(2)}) collective-permute-start(bf16[8,3,128,128]{3,2,1,0:T(8,128)(2,1)S(1)} %get-tuple-element.15.kv0), channel_id=1, source_target_pairs={{0,16},{16,0},{1,17},{17,1},{2,18},{18,2},{3,19},{19,3},{4,20},{20... | collective-permute-start | bytes 2359304 | tf_op jit(solution)/shard_map/ppermute | solution.py:330
  56.7 62.1 %collective-permute-start.9 = (bf16[8,3,64,128]{3,2,1,0:T(8,128)(2,1)S(1)}, bf16[8,3,64,128]{3,2,1,0:T(8,128)(2,1)S(1)}, u32[]{:S(2)}, u32[]{:S(2)}) collective-permute-start(bf16[8,3,64,128]{3,2,1,0:T(8,128)(2,1)S(1)} %get-tuple-element.14.q_ref), channel_id=1, source_target_pairs={{0,1},{1,0},{2,3},{3,2},{4,5},{5,4},{6,7},{7,6},{8,9},{9,8},{10,11... | collective-permute-start | bytes 1179656 | tf_op jit(solution)/shard_map/ppermute | solution.py:330
  118.9 140.7 %slice-start = ((s8[4718592]{0:T(1024)(128)(4,1)}), s8[4194304]{0:T(1024)(128)(4,1)S(1)}, s32[]{:S(2)}) async-start(s8[4718592]{0:T(1024)(128)(4,1)} %bitcast.10), calls=%async_computation.3 | async-start | bytes 8388608
  131.0 21.6 %collective-permute-start.10 = (f32[3,80,1024]{2,1,0:T(8,128)S(1)}, f32[3,80,1024]{2,1,0:T(8,128)S(1)}, u32[]{:S(2)}, u32[]{:S(2)}) collective-permute-start(f32[3,80,1024]{2,1,0:T(8,128)S(1)} %get-tuple-element.20), channel_id=1, source_target_pairs={{0,1},{1,0},{2,3},{3,2},{4,5},{5,4},{6,7},{7,6},{8,9},{9,8},{10,11... | collective-permute-start | bytes 2949128 | tf_op jit(solution)/shard_map/ppermute | solution.py:330
  131.1 21.5 %collective-permute-start = (bf16[8,3,128,128]{3,2,1,0:T(8,128)(2,1)S(1)}, bf16[8,3,128,128]{3,2,1,0:T(8,128)(2,1)S(1)}, u32[]{:S(2)}, u32[]{:S(2)}) collective-permute-start(bf16[8,3,128,128]{3,2,1,0:T(8,128)(2,1)S(1)} %get-tuple-element.15.kv0), channel_id=1, source_target_pairs={{0,1},{1,0},{2,3},{3,2},{4,5},{5,4},{6,7},{7,6},{8,9},{9,8},{10,11... | collective-permute-start | bytes 2359304 | tf_op jit(solution)/shard_map/ppermute | solution.py:330
  131.6 21.0 %collective-permute-start.2 = (bf16[8,3,128,128]{3,2,1,0:T(8,128)(2,1)S(1)}, bf16[8,3,128,128]{3,2,1,0:T(8,128)(2,1)S(1)}, u32[]{:S(2)}, u32[]{:S(2)}) collective-permute-start(bf16[8,3,128,128]{3,2,1,0:T(8,128)(2,1)S(1)} %collective-permute-done.1.kv2), channel_id=1, source_target_pairs={{0,1},{1,0},{2,3},{3,2},{4,5},{5,4},{6,7},{7,6},{8,9},{9,8},{10,11... | collective-permute-start | bytes 2359304 | tf_op jit(solution)/shard_map/ppermute | solution.py:330
  131.7 127.8 %slice-start.1 = ((s8[4718592]{0:T(1024)(128)(4,1)}), s8[524288]{0:T(1024)(128)(4,1)S(1)}, s32[]{:S(2)}) async-start(s8[4718592]{0:T(1024)(128)(4,1)} %bitcast.10), calls=%async_computation.4 | async-start | bytes 1048576
  152.6 106.9 %copy-start = (bf16[1,128,1536]{2,1,0:T(8,128)(2,1)S(1)}, bf16[1,128,1536]{2,1,0:T(8,128)(2,1)}, u32[]{:S(2)}) copy-start(bf16[1,128,1536]{2,1,0:T(8,128)(2,1)} %param.9) | copy-start | bytes 1179652
  152.6 106.9 %copy-start.1 = (f32[1,1536]{1,0:T(1,128)S(1)}, f32[1,1536]{1,0:T(1,128)}, u32[]{:S(2)}) copy-start(f32[1,1536]{1,0:T(1,128)} %gate_ref.1) | copy-start | bytes 18436
